TPU v7x, 32 devices: a whole 2x2x4 slice. The times are simulated.
32 devices in a mesh: grp: 4 (over x, core), seq: 8 (over z, y).
Axes of the slice: x: 2, y: 2, z: 4, core: 2. Of those that a mesh axis runs over, the one named last changes fastest.
Arguments:
- fields: bfloat16 [4096, 192], P(('grp', 'seq')), may hold values from -6 to 6
- patch_weight: bfloat16 [192, 1024], P(None, ('grp', 'seq')), may hold values from -3 to 3
- variable_embed: bfloat16 [48, 1024], P(None, ('grp', 'seq')), may hold values from -6 to 6
- query_vector: bfloat16 [1024], P(('grp', 'seq')), may hold values from -6 to 6
- key_weight: bfloat16 [1024, 1024], P(('grp', 'seq')), may hold values from -0.1875 to 0.1875
- value_weight: bfloat16 [1024, 1024], P(('grp', 'seq')), may hold values from -0.1875 to 0.1875
- merge_weight: bfloat16 [1024, 1024], P(('grp', 'seq')), may hold values from -0.75 to 0.75
- merge_bias: bfloat16 [1024], P(('grp', 'seq')), may hold values from -3 to 3
- position_table: bfloat16 [1024, 1024], P('seq', 'grp'), may hold values from -3 to 3
- lead_weight: bfloat16 [1024], P(('grp', 'seq')), may hold values from -6 to 6
- lead_bias: bfloat16 [1024], P(('grp', 'seq')), may hold values from -3 to 3
- first_gain: bfloat16 [1024], P(('grp', 'seq')), may hold values from 0.25 to 1.75
- first_shift: bfloat16 [1024], P(('grp', 'seq')), may hold values from -3 to 3
- joint_weight: bfloat16 [1024, 3072], P(('grp', 'seq')), may hold values from -0.1875 to 0.1875
- joint_bias: bfloat16 [2, 1024], P(None, ('grp', 'seq')), may hold values from -3 to 3
- output_weight: bfloat16 [1024, 1024], P(('grp', 'seq')), may hold values from -6 to 6
- output_bias: bfloat16 [1024], P(('grp', 'seq')), may hold values from -8 to 8
- second_gain: bfloat16 [1024], P(('grp', 'seq')), may hold values from 0.25 to 1.75
- second_shift: bfloat16 [1024], P(('grp', 'seq')), may hold values from -3 to 3
- expand_weight: bfloat16 [1024, 4096], P(('grp', 'seq')), may hold values from -0.1875 to 0.1875
- expand_bias: bfloat16 [4096], P(('grp', 'seq')), may hold values from -3 to 3
- reduce_weight: bfloat16 [4096, 1024], P(('grp', 'seq')), may hold values from -0.09375 to 0.09375
- reduce_bias: bfloat16 [1024], P(('grp', 'seq')), may hold values from -12 to 12
- segment_ids: int32 [4096], P(('grp', 'seq')), may hold values from 0 to 3, as said below
- live_rows: int32 [4096], P(('grp', 'seq')), may hold values from 0 to 1
- lead_steps: int32 [4, 4], P('grp'), may hold values from 1 to 28
- cotangent: bfloat16 [4096, 1024], P(('grp', 'seq')), may hold values from -6 to 6
Outputs:
- activations: float32 [4096, 1024], P(('grp', 'seq'))
- field_grad: float32 [4096, 192], P(('grp', 'seq'))
- grad_patch_weight: float32 [192, 1024], P(None, ('grp', 'seq'))
- grad_variable_embed: float32 [48, 1024], P(None, ('grp', 'seq'))
- grad_query_vector: float32 [1024], P(('grp', 'seq'))
- grad_key_weight: float32 [1024, 1024], P(('grp', 'seq'))
- grad_value_weight: float32 [1024, 1024], P(('grp', 'seq'))
- grad_merge_weight: float32 [1024, 1024], P(('grp', 'seq'))
- grad_merge_bias: float32 [1024], P(('grp', 'seq'))
- grad_position_table: float32 [1024, 1024], P('seq', 'grp')
- grad_lead_weight: float32 [1024], P(('grp', 'seq'))
- grad_lead_bias: float32 [1024], P(('grp', 'seq'))
- grad_first_gain: float32 [1024], P(('grp', 'seq'))
- grad_first_shift: float32 [1024], P(('grp', 'seq'))
- grad_joint_weight: float32 [1024, 3072], P(('grp', 'seq'))
- grad_joint_bias: float32 [2, 1024], P(None, ('grp', 'seq'))
- grad_output_weight: float32 [1024, 1024], P(('grp', 'seq'))
- grad_output_bias: float32 [1024], P(('grp', 'seq'))
- grad_second_gain: float32 [1024], P(('grp', 'seq'))
- grad_second_shift: float32 [1024], P(('grp', 'seq'))
- grad_expand_weight: float32 [1024, 4096], P(('grp', 'seq'))
- grad_expand_bias: float32 [4096], P(('grp', 'seq'))
- grad_reduce_weight: float32 [4096, 1024], P(('grp', 'seq'))
- grad_reduce_bias: float32 [1024], P(('grp', 'seq'))
Inputs may be any that keep to these rules, and one draw needn't show every extreme that they name: `segment_ids`: ids are compared only within a group of 1024 rows; in every group each id that occurs has rows with live_rows equal to 1.
All inputs are finite; a program needn't handle non-finite values.
Results may differ from a plain program's by a relative error of at most 0.023.
Values may be sent and summed in bfloat16 or wider, within the bound.
A program may use at most 384 MiB of HBM per device.

v0:
```python
import functools

import jax
import jax.numpy as jnp
from jax import lax
from jax.experimental import pallas as pl
from jax.experimental.pallas import tpu as pltpu
from jax.sharding import PartitionSpec as P

D = 1024
HEADS = 16
FF = 4096
VARS = 48
PIX = 4
HDIM = 64
VP = 192
KP = 256

EPSILON = 1e-05
SCALE = 0.125
LEAD_UNIT = 0.06
MASKED = -1e30

MESH = pl.DeviceIdType.MESH
ROWS = ("grp", "seq")
F32 = jnp.float32
BF16 = jnp.bfloat16


def f32(x):
    return x.astype(F32)


def low(x):
    return x.astype(BF16)


def dot(a, b, ca, cb):
    return lax.dot_general(a, b, (((ca,), (cb,)), ((), ())), preferred_element_type=F32)


def low_sums(x):
    return dot(jnp.ones((8, x.shape[0]), BF16), x, 1, 0)[0]


def exchange_kernel(axis, count, modes, *refs):
    n = len(modes)
    ins, outs = refs[:n], refs[n : 2 * n]
    send, recv, own = refs[2 * n :]
    me = lax.axis_index(axis)
    other = lax.axis_index("seq" if axis == "grp" else "grp")

    def device(index):
        return (index, other) if axis == "grp" else (other, index)

    barrier = pltpu.get_barrier_semaphore()
    for step in range(1, count):
        pl.semaphore_signal(
            barrier, inc=1, device_id=device(lax.rem(me + step, count)), device_id_type=MESH
        )
    pl.semaphore_wait(barrier, count - 1)
    copies = []
    for step in range(1, count):
        peer = lax.rem(me + step, count)
        for k in range(n):
            copy = pltpu.make_async_remote_copy(
                src_ref=ins[k] if modes[k] == "all" else ins[k].at[peer],
                dst_ref=outs[k].at[me],
                send_sem=send.at[k, step - 1],
                recv_sem=recv.at[k, step - 1],
                device_id=device(peer),
                device_id_type=MESH,
            )
            copy.start()
            copies.append(copy)
    for k in range(n):
        copy = pltpu.make_async_copy(
            ins[k] if modes[k] == "all" else ins[k].at[me], outs[k].at[me], own.at[k]
        )
        copy.start()
        copies.append(copy)
    for copy in copies:
        copy.wait()


def exchange(axis, count, ident, parts):
    arrays = [a for a, _ in parts]
    modes = tuple(m for _, m in parts)
    if ident is None:
        return [
            lax.all_gather(a, axis, axis=0, tiled=False)
            if m == "all"
            else lax.all_to_all(a, axis, 0, 0, tiled=False)
            for a, m in parts
        ]
    shapes = [
        jax.ShapeDtypeStruct(((count,) + a.shape) if m == "all" else a.shape, a.dtype)
        for a, m in parts
    ]
    n = len(parts)
    return pl.pallas_call(
        functools.partial(exchange_kernel, axis, count, modes),
        out_shape=shapes,
        in_specs=[pl.BlockSpec(memory_space=pl.ANY)] * n,
        out_specs=[pl.BlockSpec(memory_space=pl.ANY)] * n,
        scratch_shapes=[
            pltpu.SemaphoreType.DMA((n, count - 1)),
            pltpu.SemaphoreType.DMA((n, count - 1)),
            pltpu.SemaphoreType.DMA((n,)),
        ],
        compiler_params=pltpu.CompilerParams(collective_id=ident, has_side_effects=True),
    )(*arrays)


def norm_parts(x):
    center = x - jnp.mean(x, axis=-1, keepdims=True)
    spread = jnp.mean(center * center, axis=-1, keepdims=True)
    inverse = lax.rsqrt(spread + EPSILON)
    return center * inverse, inverse


def norm_back(hat, inverse, gain, grad):
    f = grad * gain
    return inverse * (
        f
        - jnp.mean(f, axis=-1, keepdims=True)
        - hat * jnp.mean(f * hat, axis=-1, keepdims=True)
    )


def pack(pieces):
    flat = jnp.concatenate([f32(p).reshape(-1) for p in pieces])
    short = -flat.shape[0] % 1024
    return jnp.pad(flat, (0, short)).reshape(-1, 128)


def unpack(table, sizes):
    flat = table.reshape(table.shape[:-2] + (-1,))
    out, at = [], 0
    for size in sizes:
        out.append(flat[..., at : at + size])
        at += size
    return out


def softmax_parts(q, k, allowed):
    scores = jnp.einsum("hqc,hkc->hqk", q, k, preferred_element_type=F32) * SCALE
    masked = jnp.where(allowed[None], scores, MASKED)
    top = jnp.max(masked, axis=-1, keepdims=True)
    terms = jnp.where(allowed[None], jnp.exp(masked - top), 0.0)
    total = jnp.sum(terms, axis=-1, keepdims=True)
    return terms * (1.0 / total)


def attend(q, k, v, allowed):
    weights = softmax_parts(q, k, allowed)
    return jnp.einsum("hqk,hkc->hqc", low(weights), v, preferred_element_type=F32)


def attend_back(q, k, v, allowed, grad, attended):
    weights = softmax_parts(q, k, allowed)
    offset = jnp.sum(f32(grad) * attended, axis=-1)
    pushed = jnp.einsum("hqc,hkc->hqk", grad, v, preferred_element_type=F32)
    slopes = low(weights * (pushed - offset[..., None])) * BF16(SCALE)
    grad_q = jnp.einsum("hqk,hkc->hqc", slopes, k, preferred_element_type=F32)
    grad_k = jnp.einsum("hqk,hqc->hkc", slopes, q, preferred_element_type=F32)
    grad_v = jnp.einsum("hqk,hqc->hkc", low(weights), grad, preferred_element_type=F32)
    return grad_q, grad_k, grad_v


def heads_first(x):
    return x.transpose(1, 0, 2)


def heads_last(x):
    return x.transpose(1, 0, 2)


def allowed_pairs(query_codes, key_codes):
    return ((query_codes[:, None] >> 1) == (key_codes[None, :] >> 1)) & (
        (key_codes[None, :] & 1) == 1
    )


def shards(
    G,
    S,
    fields,
    patch_weight,
    variable_embed,
    query_vector,
    key_weight,
    value_weight,
    merge_weight,
    merge_bias,
    position_table,
    lead_weight,
    lead_bias,
    first_gain,
    first_shift,
    joint_weight,
    joint_bias,
    output_weight,
    output_bias,
    second_gain,
    second_shift,
    expand_weight,
    expand_bias,
    reduce_weight,
    reduce_bias,
    segment_ids,
    live_rows,
    lead_steps,
    cotangent,
):
    R = fields.shape[0]
    dn = value_weight.shape[0]
    fn = reduce_weight.shape[0]
    RG = G * R
    HL = HEADS // G
    CL = HL * HDIM
    FL = FF // G
    pairs = G * HL
    direct = pairs % S == 0 and HL % max(pairs // S, 1) == 0 and dn % 16 == 0 and R % 16 == 0
    idents = iter(range(1, 100))

    def swap(axis, *parts):
        return exchange(axis, G if axis == "grp" else S, next(idents) if direct else None, parts)

    def gather_rows(w):
        return lax.all_gather(w, "seq", axis=0, tiled=True)

    merge_s = gather_rows(merge_weight)
    output_s = gather_rows(output_weight)

    table = jnp.concatenate(
        [patch_weight, variable_embed, jnp.zeros((KP - VP - VARS, dn), BF16)], axis=0
    )
    value_part = low(dot(value_weight, table, 0, 1)).reshape(G, CL, KP)
    key_part = low(dot(key_weight, table, 0, 1)).reshape(G, CL, KP)
    both = jnp.concatenate([value_part, key_part], axis=1)
    codes_own = segment_ids * 2 + live_rows
    vectors_own = [
        query_vector,
        merge_bias,
        lead_weight,
        lead_bias,
        first_gain,
        first_shift,
        output_bias,
        second_gain,
        second_shift,
        reduce_bias,
    ]
    small_own = pack([codes_own] + vectors_own)
    widen = (jnp.arange(VP)[:, None] == jnp.arange(KP)[None, :]).astype(BF16)
    column = jnp.arange(KP)
    field_own = low(dot(fields, widen, 1, 0) + ((column >= VP) & (column < VP + VARS)))
    joint_own = joint_weight.reshape(dn, 3, G, CL).transpose(2, 0, 1, 3).reshape(G, dn, 3 * CL)
    expand_own = expand_weight.reshape(dn, G, FL).transpose(1, 0, 2)
    both, joint_in, expand_in, field_in, position_in, small_in, cot_in = swap(
        "grp",
        (both, "each"),
        (joint_own, "each"),
        (expand_own, "each"),
        (field_own, "all"),
        (position_table, "all"),
        (small_own, "all"),
        (cotangent, "all"),
    )
    joint_s = (
        lax.all_gather(joint_in, "seq", axis=0, tiled=False)
        .transpose(1, 0, 2, 3)
        .reshape(D, 3 * CL)
    )
    expand_s = (
        lax.all_gather(expand_in, "seq", axis=0, tiled=False).transpose(1, 0, 2, 3).reshape(D, FL)
    )
    reduce_s = gather_rows(reduce_weight)
    field_rows = field_in.reshape(RG, KP)
    field_wide = dot(field_rows, (column[:, None] == column[None, :]).astype(BF16), 1, 0)
    cot_rows = cot_in.reshape(RG, D)
    position_rows = position_in.transpose(1, 0, 2).reshape(R, D)
    both = low(jnp.sum(f32(both), axis=0)).reshape(2, S, dn, KP).transpose(1, 0, 2, 3)
    small_rows = small_in.shape[0] * small_in.shape[1]
    slim = pack([joint_bias, expand_bias])
    both, small_all, slim_all = swap(
        "seq",
        (both.reshape(S, 2 * dn, KP), "each"),
        (small_in.reshape(small_rows, 128), "all"),
        (slim, "all"),
    )
    both = jnp.sum(f32(both), axis=0).reshape(2, dn, KP)
    value_own, key_own = both[0], both[1]
    probe_part = jnp.sum(key_own * f32(query_vector)[:, None], axis=0) * SCALE
    value_table, probe_parts = swap(
        "seq",
        (low(value_own), "all"),
        (jnp.broadcast_to(probe_part[None], (8, KP)), "all"),
    )
    value_table = value_table.reshape(CL, KP)
    probe_table = jnp.sum(probe_parts[:, 0].reshape(HL, S // HL, KP), axis=1)

    small_all = small_all.reshape(S, G, -1, 128)
    pieces = unpack(small_all, [R] + [dn] * len(vectors_own))
    codes = pieces[0].astype(jnp.int32)
    (
        full_query,
        full_merge_bias,
        full_lead,
        full_lead_bias,
        full_first_gain,
        full_first_shift,
        full_output_bias,
        full_second_gain,
        full_second_shift,
        full_reduce_bias,
    ) = [p.transpose(1, 0, 2).reshape(D) for p in pieces[1:]]
    joint_shift, expand_shift = unpack(slim_all, [2 * dn, fn])
    joint_shift = joint_shift.reshape(S, 2, dn).transpose(1, 0, 2).reshape(2, CL)
    expand_shift = expand_shift.reshape(FL)

    picked = jnp.where(
        segment_ids[:, None] == jnp.arange(lead_steps.shape[1])[None, :], lead_steps, 0
    )
    lead_rows = LEAD_UNIT * jnp.sum(picked, axis=1).astype(F32)

    owner = jnp.concatenate(
        [jnp.arange(VP) // PIX, jnp.arange(VARS), jnp.full((KP - VP - VARS,), VARS)]
    )
    select = (owner[:, None] == jnp.arange(VARS)[None, :]).astype(BF16)
    maps = probe_table[:, :, None] * f32(select)[None]
    maps_high = low(maps)
    maps_low = low(maps - f32(maps_high))
    scores = jnp.einsum("rk,hkv->hrv", field_rows, maps_high, preferred_element_type=F32)
    scores = scores + jnp.einsum("rk,hkv->hrv", field_rows, maps_low, preferred_element_type=F32)
    chosen = jax.nn.softmax(scores, axis=-1)
    spread = jnp.einsum("hrv,kv->hrk", low(chosen), select, preferred_element_type=F32)
    mixed = low(spread * field_wide[None])
    value_heads = value_table.reshape(HL, HDIM, KP)
    head_low = low(
        jnp.einsum("hrk,hck->rhc", mixed, value_heads, preferred_element_type=F32).reshape(RG, CL)
    )
    merged = low(dot(head_low, merge_s, 1, 0)).reshape(G, R, D)
    (merged,) = swap("grp", (merged, "each"))
    start = (
        jnp.sum(f32(merged), axis=0)
        + full_merge_bias
        + f32(position_rows)
        + lead_rows[:, None] * full_lead
        + full_lead_bias
    )
    start_hat, start_inv = norm_parts(start)
    (normed,) = swap("grp", (low(start_hat * full_first_gain + full_first_shift), "all"))
    normed = normed.reshape(RG, D)
    joint = dot(normed, joint_s, 1, 0)
    shift = jnp.concatenate([joint_shift[0], jnp.zeros((CL,), F32), joint_shift[1]])
    joint = low(joint + shift)

    if direct:
        per = pairs // S
        split = HL // per
        width = per * HDIM

        def to_pairs(x, kinds):
            x = x.reshape(G, R, kinds, split, width).transpose(0, 3, 1, 2, 4)
            (x,) = swap("seq", (x.reshape(S, R, kinds * width), "each"))
            return x.reshape(S * R, kinds, per, HDIM)

        def from_pairs(x, kinds):
            (x,) = swap("seq", (x.reshape(S, R, kinds * width), "each"))
            return (
                x.reshape(G, split, R, kinds, width)
                .transpose(0, 2, 3, 1, 4)
                .reshape(RG, kinds * CL)
            )

        mine = lax.axis_index("seq") // split
        pair_codes = lax.dynamic_index_in_dim(codes, mine, axis=1, keepdims=False).reshape(S * R)
        allowed = allowed_pairs(pair_codes, pair_codes)
        qkv = to_pairs(joint, 3)
        q, k, v = [heads_first(qkv[:, i]) for i in range(3)]
        attended = attend(q, k, v, allowed)
        attended_low = from_pairs(heads_last(low(attended)), 1)
    else:
        heads = joint.reshape(G, R, 3, HL, HDIM).transpose(0, 2, 3, 1, 4)
        everyone = lax.all_gather(heads[:, 1:], "seq", axis=3, tiled=True)
        all_codes = codes.transpose(1, 0, 2).reshape(G, S * R)
        my_codes = lax.dynamic_index_in_dim(codes, lax.axis_index("seq"), 0, keepdims=False)

        def forward_group(item):
            q, kv, query_codes, key_codes = item
            return attend(q, kv[0], kv[1], allowed_pairs(query_codes, key_codes))

        attended = lax.map(forward_group, (heads[:, 0], everyone, my_codes, all_codes))
        attended_low = low(attended).transpose(0, 2, 1, 3).reshape(RG, CL)

    branch = low(dot(attended_low, output_s, 1, 0)).reshape(G, R, D)
    (branch,) = swap("grp", (branch, "each"))
    middle = start + jnp.sum(f32(branch), axis=0) + full_output_bias
    middle_hat, middle_inv = norm_parts(middle)
    (second,) = swap("grp", (low(middle_hat * full_second_gain + full_second_shift), "all"))
    second = second.reshape(RG, D)
    hidden = dot(second, expand_s, 1, 0) + expand_shift
    inner = 0.7978845608028654 * (hidden + 0.044715 * hidden * hidden * hidden)
    bend = jnp.tanh(inner)
    active = low(0.5 * hidden * (1.0 + bend))
    slope = 0.5 * (1.0 + bend) + 0.5 * hidden * (1.0 - bend * bend) * 0.7978845608028654 * (
        1.0 + 3.0 * 0.044715 * hidden * hidden
    )
    reduced = low(dot(active, reduce_s, 1, 0)).reshape(G, R, D)

    grad_active = dot(cot_rows, reduce_s, 1, 1)
    grad_hidden = low(grad_active * slope)
    grad_second = low(dot(grad_hidden, expand_s, 1, 1)).reshape(G, R, D)
    grad_second, reduced = swap("grp", (grad_second, "each"), (reduced, "each"))
    activations = middle + jnp.sum(f32(reduced), axis=0) + full_reduce_bias
    grad_second = jnp.sum(f32(grad_second), axis=0)
    grad_top = f32(cotangent)
    grad_middle = grad_top + norm_back(middle_hat, middle_inv, full_second_gain, grad_second)
    grad_branch = low(grad_middle)

    def scatter_rows(w):
        return lax.psum_scatter(w, "seq", scatter_dimension=0, tiled=True)

    def scatter_mixed(w):
        cols = w.shape[1]
        w = w.reshape(G, S, dn, cols).transpose(1, 0, 2, 3).reshape(S, G * dn * cols // 1024, 1024)
        w = lax.psum_scatter(w, "seq", scatter_dimension=0, tiled=False)
        return w.reshape(G, dn, cols)

    grad_reduce_weight = f32(scatter_rows(low(dot(active, cot_rows, 0, 0))))
    grad_expand_mixed = scatter_mixed(low(dot(second, grad_hidden, 0, 0)))
    grad_expand_bias = low_sums(grad_hidden)

    (grad_branch_rows,) = swap("grp", (grad_branch, "all"))
    grad_branch_rows = grad_branch_rows.reshape(RG, D)
    grad_attended = low(dot(grad_branch_rows, output_s, 1, 1))
    grad_output_weight = f32(scatter_rows(low(dot(attended_low, grad_branch_rows, 0, 0))))
    if direct:
        pushed = heads_first(to_pairs(grad_attended, 1)[:, 0])
        grad_q, grad_k, grad_v = attend_back(q, k, v, allowed, pushed, attended)
        grads = [heads_last(low(x)) for x in (grad_q, grad_k, grad_v)]
        grad_joint = from_pairs(jnp.stack(grads, axis=1), 3)
    else:
        grad_heads = grad_attended.reshape(G, R, HL, HDIM).transpose(0, 2, 1, 3)

        def backward_group(item):
            q, kv, query_codes, key_codes, grad, done = item
            grad_q, grad_k, grad_v = attend_back(
                q, kv[0], kv[1], allowed_pairs(query_codes, key_codes), grad, done
            )
            return grad_q, jnp.stack([grad_k, grad_v], axis=0)

        grad_q, grad_kv = lax.map(
            backward_group,
            (heads[:, 0], everyone, my_codes, all_codes, grad_heads, attended),
        )
        grad_kv = lax.psum_scatter(grad_kv, "seq", scatter_dimension=3, tiled=True)
        grad_joint = low(jnp.concatenate([grad_q[:, None], grad_kv], axis=1))
        grad_joint = grad_joint.transpose(0, 3, 1, 2, 4).reshape(RG, 3 * CL)
    grad_normed = low(dot(grad_joint, joint_s, 1, 1)).reshape(G, R, D)
    (grad_normed,) = swap("grp", (grad_normed, "each"))
    grad_normed = jnp.sum(f32(grad_normed), axis=0)
    grad_joint_mixed = scatter_mixed(low(dot(normed, grad_joint, 0, 0)))
    joint_sums = low_sums(grad_joint)
    grad_start = grad_middle + norm_back(start_hat, start_inv, full_first_gain, grad_normed)
    grad_merged = low(grad_start)

    grad_merged_rows, grad_joint_in, grad_expand_in = swap(
        "grp", (grad_merged, "all"), (grad_joint_mixed, "each"), (grad_expand_mixed, "each")
    )
    grad_joint_weight = f32(
        grad_joint_in.reshape(G, dn, 3, CL).transpose(1, 2, 0, 3).reshape(dn, 3 * D)
    )
    grad_expand_weight = f32(grad_expand_in.transpose(1, 0, 2).reshape(dn, FF))
    grad_merged_rows = grad_merged_rows.reshape(RG, D)
    grad_head = low(dot(grad_merged_rows, merge_s, 1, 1))
    grad_merge_weight = f32(scatter_rows(low(dot(head_low, grad_merged_rows, 0, 0))))
    grad_heads_low = grad_head.reshape(RG, HL, HDIM)
    value_back = jnp.einsum(
        "rhc,hck->hrk", grad_heads_low, value_heads, preferred_element_type=F32
    )
    weighed = value_back * field_wide[None]
    weighed_high = low(weighed)
    weighed_low = low(weighed - f32(weighed_high))
    grad_chosen = jnp.einsum("hrk,kv->hrv", weighed_high, select, preferred_element_type=F32)
    grad_chosen = grad_chosen + jnp.einsum(
        "hrk,kv->hrv", weighed_low, select, preferred_element_type=F32
    )
    grad_scores = low(
        chosen * (grad_chosen - jnp.sum(chosen * grad_chosen, axis=-1, keepdims=True))
    )
    score_spread = jnp.einsum("hrv,kv->hrk", grad_scores, select, preferred_element_type=F32)
    field_part = jnp.sum(spread * value_back + score_spread * probe_table[:, None, :], axis=0)
    field_part = field_part.reshape(G, R, KP)
    score_sums = jnp.sum(score_spread * field_wide[None], axis=1)
    head_sums = jnp.einsum(
        "rhc,hrk->hck", grad_heads_low, mixed, preferred_element_type=F32
    ).reshape(S, dn, KP)

    column_sums = jnp.stack(
        [
            low_sums(grad_merged),
            jnp.sum(lead_rows[:, None] * grad_start, axis=0),
            jnp.sum(grad_start, axis=0),
            jnp.sum(grad_normed * start_hat, axis=0),
            jnp.sum(grad_normed, axis=0),
            low_sums(grad_branch),
            jnp.sum(grad_second * middle_hat, axis=0),
            jnp.sum(grad_second, axis=0),
            jnp.sum(grad_top, axis=0),
        ]
    )
    kinds = column_sums.shape[0]
    column_sums = jnp.pad(column_sums, ((0, -kinds % 16), (0, 0)))
    column_sums = column_sums.reshape(-1, G, CL).transpose(1, 0, 2)
    position_blocks = grad_merged.reshape(R, G, CL).transpose(1, 0, 2)
    column_sums, position_blocks, field_part = swap(
        "grp", (column_sums, "each"), (position_blocks, "each"), (field_part, "each")
    )
    grad_position_table = jnp.sum(f32(position_blocks), axis=0)
    field_grad = jnp.sum(field_part, axis=0)[:, :VP]
    column_sums = jnp.sum(column_sums, axis=0)
    team_sums = jnp.concatenate(
        [
            column_sums[:kinds].reshape(kinds, S, dn).transpose(1, 0, 2).reshape(S, kinds * dn),
            joint_sums[:CL].reshape(S, dn),
            joint_sums[2 * CL :].reshape(S, dn),
            grad_expand_bias.reshape(S, fn),
        ],
        axis=1,
    )
    wide = team_sums.shape[1]
    team_sums = jnp.pad(team_sums, ((0, 0), (0, -wide % 1024))).reshape(S, -1, 128)
    score_sums = jnp.pad(score_sums, ((0, -HL % 8), (0, 0)))
    team_sums, head_sums, score_sums = swap(
        "seq", (team_sums, "each"), (low(head_sums), "each"), (score_sums, "all")
    )
    team_sums = jnp.sum(team_sums, axis=0).reshape(-1)[:wide]
    own_sums = team_sums[: kinds * dn].reshape(kinds, dn)
    grad_joint_bias = team_sums[kinds * dn : (kinds + 2) * dn].reshape(2, dn)
    grad_expand_bias = team_sums[(kinds + 2) * dn :]
    (
        grad_merge_bias,
        grad_lead_weight,
        grad_lead_bias,
        grad_first_gain,
        grad_first_shift,
        grad_output_bias,
        grad_second_gain,
        grad_second_shift,
        grad_reduce_bias,
    ) = [own_sums[i] for i in range(kinds)]
    head_sums = jnp.sum(f32(head_sums), axis=0)
    score_sums = jnp.sum(score_sums, axis=0)
    my_head = lax.axis_index("seq") * dn // HDIM
    my_scores = lax.dynamic_index_in_dim(score_sums, my_head, axis=0, keepdims=False)
    grad_query_vector = jnp.sum(key_own * my_scores[None], axis=1) * SCALE
    (head_all,) = swap("seq", (low(head_sums), "all"))
    head_all, score_all = swap(
        "grp", (head_all.reshape(S * dn, KP), "all"), (score_sums, "all")
    )
    head_all = head_all.reshape(D, KP)
    score_all = score_all[:, :HL].reshape(HEADS, KP)
    grad_value_weight = dot(table, head_all, 0, 1)
    probe_own = low(
        jnp.sum((f32(key_weight) * full_query).reshape(dn, HEADS, HDIM), axis=-1) * SCALE
    )
    grad_table = dot(head_all, value_weight, 0, 1)
    grad_table = grad_table + jnp.einsum("hk,dh->kd", score_all, f32(probe_own))
    grad_probe = jnp.einsum("kd,hk->dh", f32(table), score_all)
    grad_key_weight = (
        grad_probe[:, :, None] * full_query.reshape(HEADS, HDIM)[None] * SCALE
    ).reshape(dn, D)
    grad_patch_weight = grad_table[:VP]
    grad_variable_embed = grad_table[VP : VP + VARS]
    return (
        activations,
        field_grad,
        grad_patch_weight,
        grad_variable_embed,
        grad_query_vector,
        grad_key_weight,
        grad_value_weight,
        grad_merge_weight,
        grad_merge_bias,
        grad_position_table,
        grad_lead_weight,
        grad_lead_bias,
        grad_first_gain,
        grad_first_shift,
        grad_joint_weight,
        grad_joint_bias,
        grad_output_weight,
        grad_output_bias,
        grad_second_gain,
        grad_second_shift,
        grad_expand_weight,
        grad_expand_bias,
        grad_reduce_weight,
        grad_reduce_bias,
    )


def solution(mesh):
    by_row = P(ROWS, None)
    by_column = P(None, ROWS)
    vector = P(ROWS)
    in_specs = (
        by_row,
        by_column,
        by_column,
        vector,
        by_row,
        by_row,
        by_row,
        vector,
        P("seq", "grp"),
        vector,
        vector,
        vector,
        vector,
        by_row,
        by_column,
        by_row,
        vector,
        vector,
        vector,
        by_row,
        vector,
        by_row,
        vector,
        vector,
        vector,
        P("grp", None),
        by_row,
    )
    out_specs = (
        by_row,
        by_row,
        by_column,
        by_column,
        vector,
        by_row,
        by_row,
        by_row,
        vector,
        P("seq", "grp"),
        vector,
        vector,
        vector,
        vector,
        by_row,
        by_column,
        by_row,
        vector,
        vector,
        vector,
        by_row,
        vector,
        by_row,
        vector,
    )
    body = functools.partial(shards, mesh.shape["grp"], mesh.shape["seq"])
    return jax.shard_map(body, mesh=mesh, in_specs=in_specs, out_specs=out_specs, check_vma=False)
```

profile of v0, /device:TPU:0, one launch (start us, length us, event | category | flops | bytes accessed | tf_op | source)
XLA Modules:
  0.0 765.4 jit_solution(5564202815060550529)
XLA Ops:
  23.2 37.4 %shard_map.442 = (bf16[4,512,256]{2,1,0:T(8,128)(2,1)}, bf16[4,32,768]{2,1,0:T(8,128)(2,1)}, bf16[4,32,1024]{2,1,0:T(8,128)(2,1)}, bf16[4,128,256]{2,1,0:T(8,128...) custom-call(bf16[4,512,256]{2,1,0:T(8,128)(2,1)} %pad_maximum_fusion.refs_0_, ...), custom_call_target="tpu_custom_call" | custom-call | tf_op jit(solution)/shard_map/pallas_call | solution.py:101
  65.2 16.8 %shard_map.443 = (bf16[8,64,256]{2,1,0:T(8,128)(2,1)}, f32[8,32,128]{2,1,0:T(8,128)}, f32[8,8,128]{2,1,0:T(8,128)}) custom-call(bf16[8,64,256]{2,1,0:T(8,128)(2,1)} %bitcast.385, f32[32,128]{1,0:T(8,128)} %bitcast.418, f32[8,128]{1,0:T(8,128)} %fusion.83.refs_2_), custom_call_target="tpu_custom_call" | custom-call | tf_op jit(solution)/shard_map/pallas_call | solution.py:101
  93.2 38.0 %all_gather.21 = bf16[256,1024]{1,0:T(8,128)(2,1)} all-gather(bf16[32,1024]{1,0:T(8,128)(2,1)S(1)} %copy-done.53), channel_id=1, replica_groups=mesh['grp'=4,'seq'=8] {'seq'}, dimensions={0}, use_global_device_ids=true | all-gather | bytes 589824 | tf_op jit(solution)/shard_map/all_gather | solution.py:231
  131.2 34.4 %all_gather.24 = bf16[256,1024]{1,0:T(8,128)(2,1)} all-gather(bf16[32,1024]{1,0:T(8,128)(2,1)S(1)} %copy-done.54), channel_id=1, replica_groups=mesh['grp'=4,'seq'=8] {'seq'}, dimensions={0}, use_global_device_ids=true | all-gather | bytes 589824 | tf_op jit(solution)/shard_map/all_gather | solution.py:231
  171.6 9.3 %shard_map.444 = (bf16[8,32,256]{2,1,0:T(8,128)(2,1)}, f32[8,8,256]{2,1,0:T(8,128)}) custom-call(bf16[32,256]{1,0:T(8,128)(2,1)} %slice.264.refs_0_, f32[8,256]{1,0:T(8,128)} %broadcast_in_dim.47.refs_1_), custom_call_target="tpu_custom_call" | custom-call | tf_op jit(solution)/shard_map/pallas_call | solution.py:101
  188.9 12.5 %shard_map.445 = bf16[4,128,1024]{2,1,0:T(8,128)(2,1)} custom-call(bf16[4,128,1024]{2,1,0:T(8,128)(2,1)} %bitcast.341), custom_call_target="tpu_custom_call" | custom-call | tf_op jit(solution)/shard_map/pallas_call | solution.py:101
  205.5 14.3 %shard_map.446 = bf16[4,128,1024]{2,1,0:T(8,128)(2,1)} custom-call(bf16[128,1024]{1,0:T(8,128)(2,1)} %get-tuple-element.169.refs_0_), custom_call_target="tpu_custom_call" | custom-call | tf_op jit(solution)/shard_map/pallas_call | solution.py:101
  234.4 17.7 %shard_map.447 = bf16[8,128,384]{2,1,0:T(8,128)(2,1)} custom-call(bf16[8,128,384]{2,1,0:T(8,128)(2,1)} %copy.294.refs_0_), custom_call_target="tpu_custom_call" | custom-call | tf_op jit(solution)/shard_map/pallas_call | solution.py:101
  257.2 9.1 %fusion.108 = (f32[2,1024]{1,0:T(2,128)S(1)}, f32[2,1024,1024]{1,2,0:T(8,128)}) fusion(pred[1024,1024]{0,1:T(8,128)(4,1)} %compare_and_fusion, bf16[1024,3,2,64]{0,3,2,1:T(8,128)(2,1)} %reshape.729), kind=kOutput, calls=%fused_computation.243 | convolution fusion | flops 278922240 | bytes 11018240 | tf_op jit(solution)/shard_map/sub | solution.py:150
  272.4 14.3 %shard_map.448 = bf16[8,128,128]{2,1,0:T(8,128)(2,1)} custom-call(bf16[8,128,128]{2,1,0:T(8,128)(2,1)} %copy.297.refs_0_), custom_call_target="tpu_custom_call" | custom-call | tf_op jit(solution)/shard_map/pallas_call | solution.py:101
  290.5 13.8 %shard_map.449 = bf16[4,128,1024]{2,1,0:T(8,128)(2,1)} custom-call(bf16[4,128,1024]{2,1,0:T(8,128)(2,1)} %bitcast.342), custom_call_target="tpu_custom_call" | custom-call | tf_op jit(solution)/shard_map/pallas_call | solution.py:101
  308.0 14.1 %shard_map.450 = bf16[4,128,1024]{2,1,0:T(8,128)(2,1)} custom-call(bf16[128,1024]{1,0:T(8,128)(2,1)} %get-tuple-element.165.refs_0_), custom_call_target="tpu_custom_call" | custom-call | tf_op jit(solution)/shard_map/pallas_call | solution.py:101
  338.5 25.4 %shard_map.451 = (bf16[4,128,1024]{2,1,0:T(8,128)(2,1)}, bf16[4,128,1024]{2,1,0:T(8,128)(2,1)}) custom-call(bf16[4,128,1024]{2,1,0:T(8,128)(2,1)} %bitcast.380, bf16[4,128,1024]{2,1,0:T(8,128)(2,1)} %bitcast.381), custom_call_target="tpu_custom_call" | custom-call | tf_op jit(solution)/shard_map/pallas_call | solution.py:101
  370.3 14.1 %shard_map.452 = bf16[4,128,1024]{2,1,0:T(8,128)(2,1)} custom-call(bf16[128,1024]{1,0:T(8,128)(2,1)} %get-tuple-element.163.refs_0_), custom_call_target="tpu_custom_call" | custom-call | tf_op jit(solution)/shard_map/pallas_call | solution.py:101
  392.8 11.1 %shard_map.453 = bf16[8,128,128]{2,1,0:T(8,128)(2,1)} custom-call(bf16[8,128,128]{2,1,0:T(8,128)(2,1)} %bitcast.388), custom_call_target="tpu_custom_call" | custom-call | tf_op jit(solution)/shard_map/pallas_call | solution.py:101
  422.5 20.1 %shard_map.454 = bf16[8,128,384]{2,1,0:T(8,128)(2,1)} custom-call(bf16[8,128,384]{2,1,0:T(8,128)(2,1)} %copy.312.refs_0_), custom_call_target="tpu_custom_call" | custom-call | tf_op jit(solution)/shard_map/pallas_call | solution.py:101
  468.3 13.0 %shard_map.455 = bf16[4,128,1024]{2,1,0:T(8,128)(2,1)} custom-call(bf16[4,128,1024]{2,1,0:T(8,128)(2,1)} %bitcast.382), custom_call_target="tpu_custom_call" | custom-call | tf_op jit(solution)/shard_map/pallas_call | solution.py:101
  506.7 39.2 %reduce-scatter.6.cloned.1.call-done = bf16[1,96,1024]{2,1,0:T(8,128)(2,1)} async-done(((bf16[8,96,1024]{2,1,0:T(8,128)(2,1)}), bf16[1,96,1024]{2,1,0:T(8,128)(2,1)}) %reduce-scatter.6.cloned.1.call-update) | async-done | bytes 196624 | tf_op jit(solution)/shard_map/reduce_scatter | solution.py:429
  547.7 68.5 %reduce-scatter.8.cloned.1.call-done = bf16[1,128,1024]{2,1,0:T(8,128)(2,1)} async-done(((bf16[8,128,1024]{2,1,0:T(8,128)(2,1)}), bf16[1,128,1024]{2,1,0:T(8,128)(2,1)}) %reduce-scatter.8.cloned.1.call-update) | async-done | bytes 262160 | tf_op jit(solution)/shard_map/reduce_scatter | solution.py:429
  616.1 18.7 %shard_map.456 = (bf16[4,128,1024]{2,1,0:T(8,128)(2,1)}, bf16[4,32,768]{2,1,0:T(8,128)(2,1)}, bf16[4,32,1024]{2,1,0:T(8,128)(2,1)}) custom-call(bf16[128,1024]{1,0:T(8,128)(2,1)} %copy-done.8, bf16[4,32,768]{2,1,0:T(8,128)(2,1)} %reshape_reduce_scatter.6.refs_1_, bf16[4,32,1024]{2,1,0:T(8,128)(2,1)} %bitcast.398), custom_call_target="tpu_custom_call" | custom-call | tf_op jit(solution)/shard_map/pallas_call | solution.py:101
  643.9 12.4 %shard_map.457 = (f32[4,16,256]{2,1,0:T(8,128)}, bf16[4,128,256]{2,1,0:T(8,128)(2,1)}, f32[4,128,256]{2,1,0:T(8,128)}) custom-call(f32[4,16,256]{2,1,0:T(8,128)} %bitcast.399, bf16[4,128,256]{2,1,0:T(8,128)(2,1)} %bitcast.383, f32[4,128,256]{2,1,0:T(8,128)} %bitcast.354), custom_call_target="tpu_custom_call" | custom-call | tf_op jit(solution)/shard_map/pallas_call | solution.py:101
  659.0 8.6 %shard_map.458 = (f32[8,8,128]{2,1,0:T(8,128)}, bf16[8,32,256]{2,1,0:T(8,128)(2,1)}, f32[8,8,256]{2,1,0:T(8,128)}) custom-call(f32[8,8,128]{2,1,0:T(8,128)} %bitcast.401, bf16[8,32,256]{2,1,0:T(8,128)(2,1)} %bitcast.392, f32[8,256]{1,0:T(8,128)} %pad.25.refs_2_), custom_call_target="tpu_custom_call" | custom-call | tf_op jit(solution)/shard_map/pallas_call | solution.py:101
  670.6 8.9 %shard_map.459 = bf16[8,32,256]{2,1,0:T(8,128)(2,1)} custom-call(bf16[32,256]{1,0:T(8,128)(2,1)} %reduce_sum.406.refs_0_), custom_call_target="tpu_custom_call" | custom-call | tf_op jit(solution)/shard_map/pallas_call | solution.py:101
  702.0 54.7 %reduce-scatter.10.cloned.1.call-done = bf16[32,1024]{1,0:T(8,128)(2,1)} async-done(((bf16[256,1024]{1,0:T(8,128)(2,1)}), bf16[32,1024]{1,0:T(8,128)(2,1)}) %reduce-scatter.10.cloned.1.call-update) | async-done | bytes 65552 | tf_op jit(solution)/shard_map/reduce_scatter | solution.py:424
  (427 shorter events, 222.9 us)
Async XLA Ops:
  7.2 214.5 %all-gather.8.cloned.1.call-start = ((), (), s32[]{:S(2)}) async-start(), calls=%async_computation.11 | async-start | bytes 1769472 | tf_op jit(solution)/shard_map/all_gather | solution.py:272
  22.1 40.1 %copy-start.88 = (bf16[32]{0:T(256)(128)(2,1)S(1)}, bf16[32]{0:T(256)(128)(2,1)}, u32[]{:S(2)}) copy-start(bf16[32]{0:T(256)(128)(2,1)} %param.30) | copy-start | bytes 196
  22.1 40.1 %copy-start.92 = (bf16[2,32]{1,0:T(2,128)(2,1)S(1)}, bf16[2,32]{1,0:T(2,128)(2,1)}, u32[]{:S(2)}) copy-start(bf16[2,32]{1,0:T(2,128)(2,1)} %param.41) | copy-start | bytes 388
  23.1 41.4 %copy-start.87 = (bf16[128]{0:T(256)(128)(2,1)S(1)}, bf16[128]{0:T(256)(128)(2,1)}, u32[]{:S(2)}) copy-start(bf16[128]{0:T(256)(128)(2,1)} %param.47) | copy-start | bytes 772
  60.6 31.9 %copy-start.93 = (s32[128]{0:T(128)S(1)}, s32[128]{0:T(128)}, u32[]{:S(2)}) copy-start(s32[128]{0:T(128)} %param.50) | copy-start | bytes 1540
  60.6 31.9 %copy-start.94 = (s32[1,4]{1,0:T(1,128)S(1)}, s32[1,4]{1,0:T(1,128)}, u32[]{:S(2)}) copy-start(s32[1,4]{1,0:T(1,128)} %param.52) | copy-start | bytes 52
  60.6 32.6 %copy-start.53 = (bf16[32,1024]{1,0:T(8,128)(2,1)S(1)}, bf16[32,1024]{1,0:T(8,128)(2,1)}, u32[]{:S(2)}) copy-start(bf16[32,1024]{1,0:T(8,128)(2,1)} %param.33) | copy-start | bytes 196612
  60.7 261.4 %all-gather.10.cloned.1.call-start = ((), (), s32[]{:S(2)}) async-start(), calls=%async_computation.12 | async-start | bytes 2359296 | tf_op jit(solution)/shard_map/all_gather | solution.py:277
  61.4 69.8 %copy-start.54 = (bf16[32,1024]{1,0:T(8,128)(2,1)S(1)}, bf16[32,1024]{1,0:T(8,128)(2,1)}, u32[]{:S(2)}) copy-start(bf16[32,1024]{1,0:T(8,128)(2,1)} %param.42) | copy-start | bytes 196612
  61.4 266.4 %all-gather.6.cloned.1.call-start = ((), (), s32[]{:S(2)}) async-start(), calls=%async_computation.5 | async-start | bytes 2359296 | tf_op jit(solution)/shard_map/all_gather | solution.py:231
  62.1 443.0 %reduce-scatter.12.cloned.1.call-start = ((), (), s32[]{:S(2)}) async-start(), calls=%async_computation.9 | async-start | bytes 589824 | tf_op jit(solution)/shard_map/reduce_scatter | solution.py:424
  63.8 118.1 %copy-start.13 = (bf16[4,128,256]{2,1,0:T(8,128)(2,1)S(1)}, bf16[4,128,256]{2,1,0:T(8,128)(2,1)}, u32[]{:S(2)}) copy-start(bf16[4,128,256]{2,1,0:T(8,128)(2,1)} %get-tuple-element.54) | copy-start | bytes 786436
  82.0 83.6 %copy-start.36 = (bf16[8,64,256]{2,1,0:T(8,128)(2,1)S(1)}, bf16[8,64,256]{2,1,0:T(8,128)(2,1)}, u32[]{:S(2)}) copy-start(bf16[8,64,256]{2,1,0:T(8,128)(2,1)} %get-tuple-element.51) | copy-start | bytes 786436
  88.5 95.3 %copy-start.42 = (f32[4,8,32]{2,1,0:T(8,128)}, f32[4,8,32]{2,1,0:T(8,128)S(1)}, u32[]{:S(2)}) copy-start(f32[4,8,32]{2,1,0:T(8,128)S(1)} %get-tuple-element.210) | copy-start | bytes 12292
  93.2 90.7 %copy-start.55 = (s32[256]{0:T(256)}, s32[256]{0:T(256)S(1)}, u32[]{:S(2)}) copy-start(s32[256]{0:T(256)S(1)} %pad_add_fusion) | copy-start | bytes 3076
  204.0 101.9 %copy-start.2 = (f32[128,4,256]{2,0,1:T(8,128)}, f32[128,4,256]{2,0,1:T(8,128)S(1)}, u32[]{:S(2)}) copy-start(f32[128,4,256]{2,0,1:T(8,128)S(1)} %get-tuple-element.172) | copy-start | bytes 1572868
  306.7 60.0 %copy-start.77 = (f32[128]{0:T(128)}, f32[128]{0:T(128)S(1)}, u32[]{:S(2)}) copy-start(f32[128]{0:T(128)S(1)} %broadcast_multiply_fusion.6) | copy-start | bytes 1540
  307.0 59.8 %copy-start.81 = (f32[128]{0:T(128)}, f32[128]{0:T(128)S(1)}, u32[]{:S(2)}) copy-start(f32[128]{0:T(128)S(1)} %add_rsqrt_fusion) | copy-start | bytes 1540
  407.5 138.4 %reduce-scatter.6.cloned.1.call-start = ((), (), s32[]{:S(2)}) async-start(), calls=%async_computation.6 | async-start | bytes 1769472 | tf_op jit(solution)/shard_map/reduce_scatter | solution.py:429
  456.3 159.8 %reduce-scatter.8.cloned.1.call-start = ((), (), s32[]{:S(2)}) async-start(), calls=%async_computation.7 | async-start | bytes 2359296 | tf_op jit(solution)/shard_map/reduce_scatter | solution.py:429
  460.7 235.9 %reduce-scatter.14.cloned.1.call-start = ((), (), s32[]{:S(2)}) async-start(), calls=%async_computation.10 | async-start | bytes 2359296 | tf_op jit(solution)/shard_map/reduce_scatter | solution.py:424
  490.0 266.7 %reduce-scatter.10.cloned.1.call-start = ((), (), s32[]{:S(2)}) async-start(), calls=%async_computation.8 | async-start | bytes 589824 | tf_op jit(solution)/shard_map/reduce_scatter | solution.py:424
  493.8 122.4 %copy-start.8 = (bf16[128,1024]{1,0:T(8,128)(2,1)}, bf16[128,1024]{1,0:T(8,128)(2,1)S(1)}, u32[]{:S(2)}) copy-start(bf16[128,1024]{1,0:T(8,128)(2,1)S(1)} %get-tuple-element.162.refs_0_) | copy-start | bytes 786436
  493.8 141.1 %copy-start.16 = (bf16[256,1024]{1,0:T(8,128)(2,1)S(1)}, bf16[256,1024]{1,0:T(8,128)(2,1)}, u32[]{:S(2)}) copy-start(bf16[256,1024]{1,0:T(8,128)(2,1)} %all_gather.21) | copy-start | bytes 1572868
  (81 other events, 706.8 us)
Sparse Core Ops, SparseCore 0:
  60.8 53.1 all-gather.7
  116.1 54.6 all-gather.9
  172.9 48.0 all-gather.5
  407.6 70.5 reduce-scatter.11
  481.8 64.0 reduce-scatter.5
  549.3 66.7 reduce-scatter.7
  619.7 68.3 reduce-scatter.13
  691.7 65.0 reduce-scatter.9
where the time goes:
time: 775 us; the launch traced here: 765 us
  Pallas kernels  290 us (37%)
  waiting for transfers between devices  164 us (21%)
  local copies, waits for them, and re-layouts  97.7 us (13%)
  matrix products  83 us (11%)
  blocking collectives  72.4 us (9%)
  other arithmetic  42 us (5%)
  between operations  16 us (2%)
    pallas_call x19, Pallas kernels, exchange(): pl.pallas_call(functools.partial(exchange_kernel, axis, count, modes), ou...  290 us
    reduce_scatter x2, waiting for transfers between devices, scatter_mixed(): w = lax.psum_scatter(w, 'seq', scatter_dimension=0, tiled=False)  108 us
    all_gather x2, blocking collectives, gather_rows(): return lax.all_gather(w, 'seq', axis=0, tiled=True)  72.4 us
    reduce_scatter x3, waiting for transfers between devices, scatter_rows(): return lax.psum_scatter(w, 'seq', scatter_dimension=0, tiled=True)  54.7 us
    dot_general x25, matrix products, dot(): lax.dot_general(a, b, (((ca,), (cb,)), ((), ())), preferred_element_type=...  47.7 us
  transfers between devices with their start and end apart: 8, of which 3 were waited for; matrix products, arithmetic and copies ran while one was open for 22% of the time, Pallas kernels for 26%

commit v1 on v0

--- a/solution.py
+++ b/solution.py
@@ -1,4 +1,4 @@
-import functools
+import types
 
 import jax
 import jax.numpy as jnp
@@ -43,73 +43,13 @@
     return dot(jnp.ones((8, x.shape[0]), BF16), x, 1, 0)[0]
 
 
-def exchange_kernel(axis, count, modes, *refs):
-    n = len(modes)
-    ins, outs = refs[:n], refs[n : 2 * n]
-    send, recv, own = refs[2 * n :]
-    me = lax.axis_index(axis)
-    other = lax.axis_index("seq" if axis == "grp" else "grp")
-
-    def device(index):
-        return (index, other) if axis == "grp" else (other, index)
-
-    barrier = pltpu.get_barrier_semaphore()
-    for step in range(1, count):
-        pl.semaphore_signal(
-            barrier, inc=1, device_id=device(lax.rem(me + step, count)), device_id_type=MESH
-        )
-    pl.semaphore_wait(barrier, count - 1)
-    copies = []
-    for step in range(1, count):
-        peer = lax.rem(me + step, count)
-        for k in range(n):
-            copy = pltpu.make_async_remote_copy(
-                src_ref=ins[k] if modes[k] == "all" else ins[k].at[peer],
-                dst_ref=outs[k].at[me],
-                send_sem=send.at[k, step - 1],
-                recv_sem=recv.at[k, step - 1],
-                device_id=device(peer),
-                device_id_type=MESH,
-            )
-            copy.start()
-            copies.append(copy)
-    for k in range(n):
-        copy = pltpu.make_async_copy(
-            ins[k] if modes[k] == "all" else ins[k].at[me], outs[k].at[me], own.at[k]
-        )
-        copy.start()
-        copies.append(copy)
-    for copy in copies:
-        copy.wait()
-
-
-def exchange(axis, count, ident, parts):
-    arrays = [a for a, _ in parts]
-    modes = tuple(m for _, m in parts)
-    if ident is None:
-        return [
-            lax.all_gather(a, axis, axis=0, tiled=False)
-            if m == "all"
-            else lax.all_to_all(a, axis, 0, 0, tiled=False)
-            for a, m in parts
-        ]
-    shapes = [
-        jax.ShapeDtypeStruct(((count,) + a.shape) if m == "all" else a.shape, a.dtype)
-        for a, m in parts
+def exchange(axis, parts):
+    return [
+        lax.all_gather(a, axis, axis=0, tiled=False)
+        if mode == "all"
+        else lax.all_to_all(a, axis, 0, 0, tiled=False)
+        for a, mode in parts
     ]
-    n = len(parts)
-    return pl.pallas_call(
-        functools.partial(exchange_kernel, axis, count, modes),
-        out_shape=shapes,
-        in_specs=[pl.BlockSpec(memory_space=pl.ANY)] * n,
-        out_specs=[pl.BlockSpec(memory_space=pl.ANY)] * n,
-        scratch_shapes=[
-            pltpu.SemaphoreType.DMA((n, count - 1)),
-            pltpu.SemaphoreType.DMA((n, count - 1)),
-            pltpu.SemaphoreType.DMA((n,)),
-        ],
-        compiler_params=pltpu.CompilerParams(collective_id=ident, has_side_effects=True),
-    )(*arrays)
 
 
 def norm_parts(x):
@@ -221,11 +161,10 @@
     CL = HL * HDIM
     FL = FF // G
     pairs = G * HL
-    direct = pairs % S == 0 and HL % max(pairs // S, 1) == 0 and dn % 16 == 0 and R % 16 == 0
-    idents = iter(range(1, 100))
+    direct = pairs % S == 0 and HL % max(pairs // S, 1) == 0
 
     def swap(axis, *parts):
-        return exchange(axis, G if axis == "grp" else S, next(idents) if direct else None, parts)
+        return exchange(axis, parts)
 
     def gather_rows(w):
         return lax.all_gather(w, "seq", axis=0, tiled=True)
@@ -603,6 +542,1418 @@
     )
 
 
+TEAM = 4
+LINE = 8
+ROW = 128
+TALL = TEAM * ROW
+GROUP = LINE * ROW
+WD = D // (TEAM * LINE)
+QC = D // TEAM
+TEAM_HEADS = HEADS // TEAM
+VECTORS = 12
+QUERY, MERGE_BIAS, LEAD_WEIGHT, LEAD_BIAS, FIRST_GAIN, FIRST_SHIFT = range(6)
+OUTPUT_BIAS, SECOND_GAIN, SECOND_SHIFT, REDUCE_BIAS = range(6, 10)
+SUM_ROWS = 24
+
+INPUTS = dict(
+    fields=pltpu.VMEM,
+    patch=pltpu.VMEM,
+    embed=pltpu.VMEM,
+    key_w=pltpu.VMEM,
+    value_w=pltpu.VMEM,
+    pack=pltpu.VMEM,
+    steps=pltpu.SMEM,
+    cot=pltpu.VMEM,
+    position=pl.ANY,
+    joint_w=pl.ANY,
+    expand_w=pl.ANY,
+    merge_w=pl.ANY,
+    output_w=pl.ANY,
+    reduce_w=pl.ANY,
+)
+
+OUTPUTS = dict(
+    activations=((ROW, D), F32),
+    field_grad=((VP, ROW), F32),
+    g_patch=((WD, VP), F32),
+    g_embed=((WD, VARS), F32),
+    g_key=((WD, D), F32),
+    g_value=((WD, D), F32),
+    g_merge=((WD, D), F32),
+    g_position=((ROW, QC), F32),
+    g_joint=((WD, 3 * D), F32),
+    g_output=((WD, D), F32),
+    g_expand=((WD, FF), F32),
+    g_reduce=((ROW, D), F32),
+    small=((32, 128), F32),
+)
+
+SCRATCH = dict(
+    head_all=((TEAM, LINE, WD, KP), BF16),
+    score_all=((TEAM, 8, KP), F32),
+    score_rows=((16, KP), F32),
+    key_own=((WD, KP), F32),
+    sums=((SUM_ROWS, QC), F32),
+    pe=((WD, KP), BF16),
+    field_all=((TEAM, ROW, KP), BF16),
+    pos=((ROW, D), BF16),
+    cot_all=((TEAM, ROW, D), BF16),
+    pack_all=((LINE, TEAM, 32, 128), BF16),
+    vecs=((16, D), F32),
+    shift_e=((8, D), F32),
+    seg_q=((16, GROUP), BF16),
+    seg_k=((16, GROUP), BF16),
+    merge_s=((LINE, WD, D), BF16),
+    output_s=((LINE, WD, D), BF16),
+    reduce_s=((LINE, ROW, D), BF16),
+    joint_s=((TEAM, LINE, WD, 3 * QC), BF16),
+    expand_s=((TEAM, LINE, WD, D), BF16),
+    e2_send=((2, LINE, WD, KP), BF16),
+    e2_recv=((LINE, 2, WD, KP), BF16),
+    pv=((LINE, WD, KP), BF16),
+    at=((LINE, 8, KP), F32),
+    probe=((8, KP), F32),
+    select=((KP, 128), BF16),
+    select_t=((128, KP), BF16),
+    chosen=((TEAM_HEADS, TALL, 128), F32),
+    mixed=((TEAM_HEADS, TALL, KP), BF16),
+    head_low=((TALL, QC), BF16),
+    start=((ROW, D), F32),
+    start_hat=((ROW, D), F32),
+    start_inv=((ROW, 128), F32),
+    middle=((ROW, D), F32),
+    middle_hat=((ROW, D), F32),
+    middle_inv=((ROW, 128), F32),
+    grad_mid=((ROW, D), F32),
+    normed_all=((TEAM, ROW, D), BF16),
+    second_all=((TEAM, ROW, D), BF16),
+    gb_all=((TEAM, ROW, D), BF16),
+    gm_all=((TEAM, ROW, D), BF16),
+    pair_send=((LINE, 3, ROW, 128), BF16),
+    qkv=((3, GROUP, 128), BF16),
+    p_low=((2, GROUP, GROUP), BF16),
+    att_f=((GROUP, 128), F32),
+    att_low=((GROUP, 128), BF16),
+    att_all=((TEAM, ROW, QC), BF16),
+    g_send=((TEAM, 2, ROW, 128), BF16),
+    go=((GROUP, 128), BF16),
+    dk=((GROUP, 128), F32),
+    dv=((GROUP, 128), F32),
+    d_all=((TEAM, 3, ROW, QC), BF16),
+    active_all=((TEAM, ROW, D), BF16),
+    gh_all=((TEAM, ROW, D), BF16),
+    own_a=((ROW, D), F32),
+    own_b=((ROW, D), F32),
+    far_a=((ROW, D), F32),
+    far_b=((ROW, D), F32),
+    gw_merge=((LINE, WD, D), BF16),
+    gw_output=((LINE, WD, D), BF16),
+    gw_reduce=((LINE, ROW, D), BF16),
+    gw_joint=((TEAM, LINE, WD, 3 * QC), BF16),
+    gw_expand=((TEAM, LINE, WD, D), BF16),
+    yr_merge=((4, WD, D), BF16),
+    yr_output=((4, WD, D), BF16),
+    yr_reduce=((4, ROW, D), BF16),
+    yr_joint=((4, TEAM, WD, 3 * QC), BF16),
+    yr_expand=((4, TEAM, WD, D), BF16),
+    zr_merge=((3, WD, D), BF16),
+    za_merge=((2, WD, D), BF16),
+    zr_output=((3, WD, D), BF16),
+    za_output=((2, WD, D), BF16),
+    zr_reduce=((3, ROW, D), BF16),
+    za_reduce=((2, ROW, D), BF16),
+    zr_joint=((3, TEAM, WD, 3 * QC), BF16),
+    za_joint=((2, TEAM, WD, 3 * QC), BF16),
+    zr_expand=((3, TEAM, WD, D), BF16),
+    za_expand=((2, TEAM, WD, D), BF16),
+    xs_joint=((TEAM, WD, 3 * QC), BF16),
+    xs_expand=((TEAM, WD, D), BF16),
+    xr_joint=((TEAM, WD, 3 * QC), BF16),
+    xr_expand=((TEAM, WD, D), BF16),
+    csum=((16, D), F32),
+    crecv=((TEAM, 16, QC), F32),
+    tsum=((LINE, SUM_ROWS, QC), F32),
+    f_own=((TEAM, ROW, KP), F32),
+    f_recv=((3, ROW, KP), F32),
+    t_send=((LINE, WD, KP), BF16),
+    t_recv=((LINE, WD, KP), BF16),
+    q_all=((LINE, 8, KP), F32),
+)
+
+TEAM_SUMS = dict(
+    both=(2 * QC, KP),
+    merge=(ROW, D),
+    branch=(ROW, D),
+    second=(ROW, D),
+    reduced=(ROW, D),
+    normed=(ROW, D),
+)
+
+
+def team_sum_buffers(shape):
+    near = ((2,) + shape, BF16)
+    one = (shape, BF16)
+    return (near, near, one, one)
+
+
+SEMAPHORES = 304
+
+
+def nn(a, b):
+    return dot(a, b, 1, 0)
+
+
+def nt(a, b):
+    return dot(a, b, 1, 1)
+
+
+def tn(a, b):
+    return dot(a, b, 0, 0)
+
+
+def lanes(at, size):
+    return pl.ds(pl.multiple_of(at, 128), size)
+
+
+def rows(at, size):
+    return pl.ds(pl.multiple_of(at, size), size)
+
+
+def fused_kernel(*refs):
+    n_in, n_out = len(INPUTS), len(OUTPUTS)
+    results = types.SimpleNamespace(**dict(zip(OUTPUTS, refs[n_in : n_in + n_out])))
+    names = list(INPUTS) + list(SCRATCH) + list(OUTPUTS)
+    rest = refs[:n_in] + refs[n_in + n_out :]
+    ref = types.SimpleNamespace(**dict(zip(names, rest)))
+    rest = rest[len(names) :]
+    send, recv = rest[-2:]
+    sums = dict(zip(TEAM_SUMS, [rest[4 * i : 4 * i + 4] for i in range(len(TEAM_SUMS))]))
+    sums = types.SimpleNamespace(**sums)
+    g = lax.axis_index("grp")
+    s = lax.axis_index("seq")
+    sib = g + 1 - 2 * lax.rem(g, 2)
+    far = lax.rem(g + 2, TEAM)
+    diag = lax.rem(sib + 2, TEAM)
+    z = s // 2
+    y = s - 2 * z
+    beside = s + 1 - 2 * y
+    mine = lax.rem(3 * z, TEAM)
+    is_middle = (z == 1) | (z == 2)
+    is_end = (z == 0) | (z == 3)
+    partner = s + 2 - 4 * lax.rem(z, 2)
+    facing = lax.rem(s + 6 - 4 * z + LINE, LINE)
+    near_places = [4 * (z // 2) + y + 2 * i for i in range(2)]
+    far_places = [4 * (1 - z // 2) + y + 2 * i for i in range(2)]
+
+    def to_team(j):
+        return (j, s)
+
+    def to_line(j):
+        return (g, j)
+
+    used = [0]
+    begun = []
+
+    def reserve(count):
+        at = used[0]
+        used[0] += count
+        assert used[0] <= SEMAPHORES
+        return at
+
+    def remote(src, dst, device, at):
+        return pltpu.make_async_remote_copy(
+            src_ref=src,
+            dst_ref=dst,
+            send_sem=send.at[at],
+            recv_sem=recv.at[at],
+            device_id=device,
+            device_id_type=MESH,
+        )
+
+    def push(src, dst, device):
+        copy = remote(src, dst, device, reserve(1))
+        copy.start()
+        begun.append(copy)
+        return copy
+
+    barrier = pltpu.get_barrier_semaphore()
+    for step in range(1, TEAM):
+        pl.semaphore_signal(
+            barrier, inc=1, device_id=to_team(lax.rem(g + step, TEAM)), device_id_type=MESH
+        )
+    for step in range(1, LINE):
+        pl.semaphore_signal(
+            barrier, inc=1, device_id=to_line(lax.rem(s + step, LINE)), device_id_type=MESH
+        )
+
+    def spread(buf):
+        half = buf.shape[1] // 2
+        across = []
+        for h in range(2):
+            part = buf.at[g, pl.ds(h * half, half)]
+            across.append(push(part, part, to_team(far)))
+        return push(buf.at[g], buf.at[g], to_team(sib)), across
+
+    def spread_on(buf, across):
+        half = buf.shape[1] // 2
+        handed = []
+        for h in range(2):
+            across[h].wait_recv()
+            part = buf.at[far, pl.ds(h * half, half)]
+            handed.append(push(part, part, to_team(sib)))
+        return handed
+
+    def wait_all(copies):
+        for copy in copies:
+            copy.wait_recv()
+
+    class TeamSum:
+        def __init__(self, buffers):
+            self.ps, self.r, self.t, self.x = buffers
+            self.near_copies = [None, None]
+
+        def near(self, slot, value=None):
+            if value is not None:
+                self.ps[slot] = low(value)
+            self.near_copies[slot] = push(self.ps.at[slot], self.r.at[slot], to_team(sib))
+
+        def across(self, value):
+            self.near_copies[1].wait_recv()
+            half = self.t.shape[0] // 2
+            self.far_copies = []
+            for h in range(2):
+                part = pl.ds(h * half, half)
+                self.t[part] = low(value(part) + f32(self.r[1, part]))
+                self.far_copies.append(push(self.t.at[part], self.x.at[part], to_team(far)))
+
+        def total(self, own):
+            self.near_copies[0].wait_recv()
+            wait_all(self.far_copies)
+            return own + f32(self.r[0]) + f32(self.x[...])
+
+    deposits = []
+
+    def deposit(src, dst):
+        copy = pltpu.make_async_copy(src, dst, recv.at[reserve(1)])
+        copy.start()
+        deposits.append(copy)
+
+    def share_line(src, dst):
+        return [push(src, dst, to_line(lax.rem(s + step, LINE))) for step in range(1, LINE)]
+
+    def mean(x):
+        return jnp.sum(x, axis=-1, keepdims=True) * (1.0 / D)
+
+    class Gather:
+        def __init__(self, slot):
+            self.slot = slot
+            self.at = reserve(9)
+
+        def send(self, place, device, i, shard=None):
+            part = self.slot(place)
+            remote(part if shard is None else shard, part, device, self.at + i).start()
+
+        def come(self, i):
+            part = self.slot(s)
+            remote(part, part, to_line(beside), self.at + i).wait_recv()
+
+        def stage1(self, shard=None):
+            self.send(s, to_line(partner), 0, shard)
+            self.send(s, to_line(beside), 1, shard)
+
+        def stage2(self):
+            self.come(0)
+
+            @pl.when(is_middle)
+            def _():
+                for i in range(2):
+                    self.send(near_places[i], to_line(facing), 2 + i)
+
+            self.send(partner, to_line(beside), 4)
+
+        def stage3(self):
+            @pl.when(is_middle)
+            def _():
+                for i in range(2):
+                    self.come(2 + i)
+                    self.send(far_places[i], to_line(partner), 5 + i)
+                    self.send(far_places[i], to_line(beside), 7 + i)
+
+        def stage4(self):
+            @pl.when(is_end)
+            def _():
+                for i in range(2):
+                    self.come(5 + i)
+                    self.send(far_places[i], to_line(beside), 7 + i)
+
+        def finish(self):
+            for i in (1, 4, 7, 8):
+                self.come(i)
+
+        def sent(self):
+            part = self.slot(s)
+
+            def gone(i):
+                remote(part, part, to_line(beside), self.at + i).wait_send()
+
+            for i in (0, 1, 4, 7, 8):
+                gone(i)
+
+            @pl.when(is_middle)
+            def _():
+                for i in (2, 3, 5, 6):
+                    gone(i)
+
+    pe = ref.pe
+    pe[:, 0:VP] = ref.patch[...]
+    pe[:, VP : VP + VARS] = ref.embed[...]
+    pe[:, VP + VARS :] = jnp.zeros((WD, KP - VP - VARS), BF16)
+    field_all, cot_all, pack_all = ref.field_all, ref.cot_all, ref.pack_all
+    field_all[g, :, 0:VP] = ref.fields[...].T
+    lane = lax.broadcasted_iota(jnp.int32, (ROW, KP - VP), 1)
+    field_all[g, :, VP:] = (lane < VARS).astype(BF16)
+    cot_all[g] = ref.cot[...]
+    pack_all[s, g] = ref.pack[...]
+    pl.semaphore_wait(barrier, TEAM - 1 + LINE - 1)
+
+    both = TeamSum(sums.both)
+
+    def table_product(weight, j):
+        return tn(weight[:, lanes(j * QC, QC)], pe[...])
+
+    for slot, j in ((1, diag), (0, sib)):
+        both.ps[slot, 0:QC] = low(table_product(ref.value_w, j))
+        both.ps[slot, QC:] = low(table_product(ref.key_w, j))
+        both.near(slot)
+    field_copies = spread(field_all)
+    far_parts = [table_product(ref.value_w, far), table_product(ref.key_w, far)]
+    both.across(lambda part: far_parts[0] if part.start == 0 else far_parts[1])
+    own_parts = [table_product(ref.value_w, g), table_product(ref.key_w, g)]
+    pack_copies = [
+        push(pack_all.at[s, g], pack_all.at[s, g], to_team(j)) for j in (far, diag, sib)
+    ]
+
+    def whole(buf):
+        return lambda i: buf.at[i]
+
+    def inner(buf):
+        return lambda i: buf.at[:, i]
+
+    gather_merge = Gather(whole(ref.merge_s))
+    gather_output = Gather(whole(ref.output_s))
+    gather_reduce = Gather(whole(ref.reduce_s))
+    gather_joint = Gather(inner(ref.joint_s))
+    gather_expand = Gather(inner(ref.expand_s))
+    local = []
+
+    def keep(src, dst):
+        copy = pltpu.make_async_copy(src, dst, recv.at[reserve(1)])
+        copy.start()
+        local.append(copy)
+
+    keep(ref.merge_w, ref.merge_s.at[s])
+    keep(ref.output_w, ref.output_s.at[s])
+    keep(ref.reduce_w, ref.reduce_s.at[s])
+    gather_merge.stage1(ref.merge_w)
+    gather_output.stage1(ref.output_w)
+    gather_reduce.stage1(ref.reduce_w)
+
+    joint_copies, expand_copies = [], []
+    for j in (far, diag, sib):
+        for kind in range(3):
+            joint_copies.append(
+                push(
+                    ref.joint_w.at[:, lanes(kind * D + j * QC, QC)],
+                    ref.joint_s.at[g, s, :, pl.ds(kind * QC, QC)],
+                    to_team(j),
+                )
+            )
+    for kind in range(3):
+        keep(
+            ref.joint_w.at[:, lanes(kind * D + g * QC, QC)],
+            ref.joint_s.at[g, s, :, pl.ds(kind * QC, QC)],
+        )
+    for j in (far, diag, sib):
+        expand_copies.append(
+            push(ref.expand_w.at[:, lanes(j * D, D)], ref.expand_s.at[g, s], to_team(j))
+        )
+    keep(ref.expand_w.at[:, lanes(g * D, D)], ref.expand_s.at[g, s])
+    keep(ref.position, ref.pos.at[:, lanes(g * QC, QC)])
+    position_copies = [
+        push(ref.position, ref.pos.at[:, lanes(g * QC, QC)], to_team(j))
+        for j in (far, diag, sib)
+    ]
+
+    both.near_copies[0].wait_recv()
+    wait_all(both.far_copies)
+    for part in range(2):
+        block = pl.ds(part * QC, QC)
+        total = own_parts[part] + f32(both.r[0, block]) + f32(both.x[block])
+        ref.e2_send[part] = low(total).reshape(LINE, WD, KP)
+    e2_send, e2_recv = ref.e2_send, ref.e2_recv
+    e2_copies = []
+    for step in range(1, LINE):
+        to = lax.rem(s + step, LINE)
+        e2_copies.append(push(e2_send.at[:, to], e2_recv.at[s], to_line(to)))
+    e2_recv[s] = e2_send[:, s]
+    for copy in local:
+        copy.wait()
+    gather_merge.stage2()
+    gather_output.stage2()
+    wait_all(joint_copies)
+    gather_joint.stage1()
+
+    wait_all(e2_copies)
+    table_own = jnp.sum(f32(e2_recv[...]), axis=0)
+    key_own = table_own[1]
+    ref.key_own[...] = key_own
+    query = f32(pack_all[s, g])[0:1, 0:WD]
+    key_high = low(key_own)
+    key_rest = low(key_own - f32(key_high))
+    query_rows = low(jnp.broadcast_to(query, (16, WD)))
+    probe_part = (nn(query_rows, key_high) + nn(query_rows, key_rest)) * SCALE
+    pv, at = ref.pv, ref.at
+    pv[s] = low(table_own[0])
+    at[s] = probe_part[0:8]
+    pv_copies = share_line(pv.at[s], pv.at[s])
+    at_copies = share_line(at.at[s], at.at[s])
+    gather_merge.stage3()
+    gather_output.stage3()
+    wait_all(pv_copies)
+    wait_all(at_copies)
+    gather_joint.stage2()
+    wait_all(pack_copies)
+    pack_line = share_line(pack_all.at[s], pack_all.at[s])
+    gather_merge.stage4()
+    gather_reduce.stage2()
+
+    probe = ref.probe
+    for h in range(TEAM_HEADS):
+        probe[h : h + 1] = at[2 * h, 0:1] + at[2 * h + 1, 0:1]
+    probe[TEAM_HEADS:] = jnp.zeros((8 - TEAM_HEADS, KP), F32)
+
+    def owner_of(k):
+        return jnp.where(k < VP, k // PIX, jnp.where(k < VP + VARS, k - VP, VARS + 64))
+
+    select, select_t = ref.select, ref.select_t
+    select[...] = (
+        owner_of(lax.broadcasted_iota(jnp.int32, (KP, 128), 0))
+        == lax.broadcasted_iota(jnp.int32, (KP, 128), 1)
+    ).astype(BF16)
+    select_t[...] = (
+        owner_of(lax.broadcasted_iota(jnp.int32, (128, KP), 1))
+        == lax.broadcasted_iota(jnp.int32, (128, KP), 0)
+    ).astype(BF16)
+    valid = lax.broadcasted_iota(jnp.int32, (1, 128), 1) < VARS
+    head_of_lane = lax.broadcasted_iota(jnp.int32, (1, QC), 1) // HDIM
+
+    field_handed = spread_on(field_all, field_copies[1])
+    field_copies[0].wait_recv()
+    wait_all(field_handed)
+
+    def tall(buf):
+        return buf[...].reshape(TALL, -1)
+
+    def split_dot(x, b):
+        high = low(x)
+        return nn(high, b) + nn(low(x - f32(high)), b)
+
+    chosen, mixed, head_low = ref.chosen, ref.mixed, ref.head_low
+
+    def choose(h):
+        field = f32(tall(field_all))
+        scores = split_dot(field * probe[h : h + 1], select[...])
+        scores = jnp.where(valid, scores, MASKED)
+        terms = jnp.exp(scores - jnp.max(scores, axis=-1, keepdims=True))
+        weights = terms * (1.0 / jnp.sum(terms, axis=-1, keepdims=True))
+        chosen[h] = weights
+        mix = low(nn(low(weights), select_t[...]) * field)
+        mixed[h] = mix
+        table_value = pv[2 * h : 2 * h + 2].reshape(HDIM, KP)
+        head_low[:, h * HDIM : (h + 1) * HDIM] = low(nt(mix, table_value))
+
+    for h in range(TEAM_HEADS):
+        choose(h)
+        if h == 1:
+            gather_joint.stage3()
+            wait_all(expand_copies)
+            gather_expand.stage1()
+
+    merge_s, output_s = ref.merge_s, ref.output_s
+    gather_output.stage4()
+    gather_merge.finish()
+    merge = TeamSum(sums.merge)
+
+    def row_weight(buf):
+        return buf[...].reshape(-1, D)
+
+    def two(buf, i, j):
+        return jnp.concatenate([buf[i], buf[j]], axis=0)
+
+    def merge_part(j):
+        return nn(head_low[rows(j * ROW, ROW)], row_weight(merge_s))
+
+    merge.near(1, merge_part(diag))
+    merge.near(0, merge_part(sib))
+    ref.far_a[...] = merge_part(far)
+    merge.across(lambda part: ref.far_a[part])
+    ref.own_a[...] = merge_part(g)
+
+    wait_all(pack_line)
+    vecs, shift_e = ref.vecs, ref.shift_e
+    place = (
+        (lax.broadcasted_iota(jnp.int32, (128, QC), 1) % WD)
+        == lax.broadcasted_iota(jnp.int32, (128, QC), 0)
+    ).astype(BF16)
+    lane_piece = lax.broadcasted_iota(jnp.int32, (LINE, 1, QC), 2) // WD
+    piece = lax.broadcasted_iota(jnp.int32, (LINE, 1, QC), 0)
+    for j in range(TEAM):
+        spreadout = nn(pack_all[:, j, 0:16, :].reshape(LINE * 16, 128), place)
+        spreadout = jnp.where(lane_piece == piece, spreadout.reshape(LINE, 16, QC), 0.0)
+        vecs[:, j * QC : (j + 1) * QC] = jnp.sum(spreadout, axis=0)
+
+    def vector(i):
+        return vecs[i : i + 1, :]
+
+    joint_shift = vecs[10:12, lanes(g * QC, QC)]
+    seg_q, seg_k = ref.seg_q, ref.seg_k
+    sub = lax.broadcasted_iota(jnp.int32, (16, 128), 0).astype(F32)
+    for j in range(LINE):
+        part = f32(pack_all[j, g])
+        shift_e[:, j * 128 : (j + 1) * 128] = jnp.broadcast_to(part[16:17], (8, 128))
+        part = f32(pack_all[j, mine])
+        same = jnp.where(sub == part[17:18], 1.0, 0.0)
+        seg_q[:, j * 128 : (j + 1) * 128] = low(same)
+        seg_k[:, j * 128 : (j + 1) * 128] = low(same * part[18:19])
+    own_seg = f32(ref.pack[...])[17:18]
+    steps = ref.steps
+    lead_lanes = jnp.zeros((1, 128), F32)
+    for i in range(steps.shape[1]):
+        lead_lanes = jnp.where(own_seg == i, LEAD_UNIT * steps[0, i].astype(F32), lead_lanes)
+    lead = jnp.broadcast_to(lead_lanes, (ROW, 128)).T[:, 0:1]
+    wait_all(position_copies)
+
+    start_ref = ref.start
+    start_ref[...] = (
+        merge.total(ref.own_a[...])
+        + vector(MERGE_BIAS)
+        + f32(ref.pos[...])
+        + lead * vector(LEAD_WEIGHT)
+        + vector(LEAD_BIAS)
+    )
+
+    def norm(x, hat_ref, inv_ref, gain, shift):
+        center = x - mean(x)
+        inverse = lax.rsqrt(mean(center * center) + EPSILON)
+        hat = center * inverse
+        hat_ref[...] = hat
+        inv_ref[...] = jnp.broadcast_to(inverse, (ROW, 128))
+        return low(hat * gain + shift)
+
+    def norm_back_ref(grad, hat_ref, inv_ref, gain):
+        f = grad * gain
+        hat = hat_ref[...]
+        return inv_ref[:, 0:1] * (f - mean(f) - hat * mean(f * hat))
+
+    normed_all = ref.normed_all
+    normed_all[g] = norm(
+        start_ref[...],
+        ref.start_hat,
+        ref.start_inv,
+        vector(FIRST_GAIN),
+        vector(FIRST_SHIFT),
+    )
+    normed_copies = spread(normed_all)
+    joint_s, pair_send, qkv = ref.joint_s, ref.pair_send, ref.qkv
+    gather_joint.stage4()
+    gather_reduce.stage3()
+    gather_expand.stage2()
+    gather_joint.finish()
+    e6 = reserve(LINE)
+
+    def pair_place(j, t):
+        return 2 * lax.rem(3 * j, TEAM) + t
+
+    def to_pair(src, dst, base, j, t):
+        there = pair_place(j, t)
+        index = base + lax.rem(there - s + LINE, LINE)
+
+        @pl.when(there != s)
+        def _():
+            remote(src, dst, to_line(there), index).start()
+
+        @pl.when(there == s)
+        def _():
+            pltpu.make_async_copy(src, dst, recv.at[index]).start()
+
+    def pairs_done(src, dst, base):
+        pltpu.make_async_copy(src, dst, recv.at[base]).wait()
+        for step in range(1, LINE):
+            copy = remote(src, dst, to_line(lax.rem(s + step, LINE)), base + step)
+            copy.wait_recv()
+            copy.wait_send()
+
+    line_rows = rows(s * ROW, ROW)
+
+    def joint_rows(i, j):
+        block = two(normed_all, i, j)
+        for kind in range(3):
+            weight = joint_s[:, :, :, kind * QC : (kind + 1) * QC].reshape(D, QC)
+            part = nn(block, weight)
+            if kind != 1:
+                part = part + joint_shift[kind // 2 : kind // 2 + 1]
+            part = low(part)
+            for n, group in enumerate((i, j)):
+                for t in range(2):
+                    pair_send[2 * group + t, kind] = part[
+                        n * ROW : (n + 1) * ROW, t * 128 : (t + 1) * 128
+                    ]
+        for group in (i, j):
+            for t in range(2):
+                to_pair(pair_send.at[2 * group + t], qkv.at[:, line_rows, :], e6, group, t)
+
+    normed_copies[0].wait_recv()
+    joint_rows(g, sib)
+    normed_handed = spread_on(normed_all, normed_copies[1])
+    wait_all(normed_handed)
+    joint_rows(far, diag)
+    pairs_done(pair_send.at[0], qkv.at[:, line_rows, :], e6)
+    gather_reduce.stage4()
+    gather_expand.stage3()
+    cot_copies = spread(cot_all)
+
+    half_of_lane = lax.broadcasted_iota(jnp.int32, (1, 128), 1) // HDIM
+    p_low, att_f, att_low, att_all = ref.p_low, ref.att_f, ref.att_low, ref.att_all
+    e7 = reserve(LINE)
+    pair_lanes = lanes(y * 128, 128)
+
+    def attend_rows(b, carry):
+        here = rows(b * 256, 256)
+        queries = f32(qkv[0, here, :]) * SCALE
+        keys, values = qkv[1], qkv[2]
+        allowed = tn(seg_q[:, lanes(b * 256, 256)], seg_k[...]) > 0.5
+        outs = []
+        for t in range(2):
+            scores = nt(low(jnp.where(half_of_lane == t, queries, 0.0)), keys)
+            scores = jnp.where(allowed, scores, MASKED)
+            terms = jnp.exp(scores - jnp.max(scores, axis=-1, keepdims=True))
+            weights = low(terms * (1.0 / jnp.sum(terms, axis=-1, keepdims=True)))
+            p_low[t, here, :] = weights
+            outs.append(nn(weights, values))
+        out = jnp.where(half_of_lane == 0, outs[0], outs[1])
+        att_f[here] = out
+        att_low[here] = low(out)
+        for t in range(2):
+            there = 2 * b + t
+            index = e7 + lax.rem(there - s + LINE, LINE)
+            src = att_low.at[rows(there * ROW, ROW)]
+            dst = att_all.at[mine, :, pair_lanes]
+
+            @pl.when(there != s)
+            def _():
+                remote(src, dst, to_line(there), index).start()
+
+            @pl.when(there == s)
+            def _():
+                pltpu.make_async_copy(src, dst, recv.at[index]).start()
+
+        return carry
+
+    lax.fori_loop(0, GROUP // 256, attend_rows, 0)
+    gather_output.finish()
+    pairs_done(att_low.at[pl.ds(0, ROW)], att_all.at[mine, :, pair_lanes], e7)
+
+    gather_expand.stage4()
+    branch = TeamSum(sums.branch)
+
+    def branch_part(j):
+        return nn(att_all[j], row_weight(output_s))
+
+    branch.near(1, branch_part(diag))
+    branch.near(0, branch_part(sib))
+    ref.far_a[...] = branch_part(far)
+    branch.across(lambda part: ref.far_a[part])
+    ref.own_a[...] = branch_part(g)
+    cot_handed = spread_on(cot_all, cot_copies[1])
+    middle_ref = ref.middle
+    middle_ref[...] = branch.total(ref.own_a[...]) + start_ref[...] + vector(OUTPUT_BIAS)
+
+    second_all = ref.second_all
+    second_all[g] = norm(
+        middle_ref[...],
+        ref.middle_hat,
+        ref.middle_inv,
+        vector(SECOND_GAIN),
+        vector(SECOND_SHIFT),
+    )
+    second_copies = spread(second_all)
+    gather_expand.finish()
+    gather_reduce.finish()
+    cot_copies[0].wait_recv()
+    wait_all(cot_handed)
+    expand_s, reduce_s = ref.expand_s, ref.reduce_s
+    active_all, gh_all = ref.active_all, ref.gh_all
+    root = 0.7978845608028654
+
+    def feed(j, k, acc_a, acc_b):
+        def tile(i, carry):
+            here = lanes(i * 256, 256)
+            up = expand_s[:, :, :, here].reshape(D, 256)
+            down = reduce_s[pl.ds(2 * i, 2)].reshape(256, D)
+            hidden = nn(two(second_all, j, k), up) + shift_e[0:1, here]
+            square = hidden * hidden
+            bend = jnp.tanh(root * hidden * (1.0 + 0.044715 * square))
+            active = low(0.5 * hidden * (1.0 + bend))
+            slope = 0.5 * (1.0 + bend) + (0.5 * root) * hidden * (1.0 - bend * bend) * (
+                1.0 + (3.0 * 0.044715) * square
+            )
+            grad = low(nt(two(cot_all, j, k), down) * slope)
+            for n, block in enumerate((j, k)):
+                active_all[block, :, here] = active[n * ROW : (n + 1) * ROW]
+                gh_all[block, :, here] = grad[n * ROW : (n + 1) * ROW]
+            for part, acc in ((nt(grad, up), acc_a), (nn(active, down), acc_b)):
+                for n in range(2):
+                    rows_of = part[n * ROW : (n + 1) * ROW]
+
+                    @pl.when(i == 0)
+                    def _():
+                        acc[n][...] = rows_of
+
+                    @pl.when(i > 0)
+                    def _():
+                        acc[n][...] += rows_of
+
+            return carry
+
+        lax.fori_loop(0, FF // TEAM // 256, tile, 0)
+
+    second = TeamSum(sums.second)
+    reduced = TeamSum(sums.reduced)
+    own_a, own_b, far_a, far_b = ref.own_a, ref.own_b, ref.far_a, ref.far_b
+    spare_a, spare_b = ref.grad_mid, ref.activations
+    second_copies[0].wait_recv()
+    feed(g, sib, (own_a, spare_a), (own_b, spare_b))
+    second.near(0, spare_a[...])
+    reduced.ps[0] = low(spare_b[...])
+    second_handed = spread_on(second_all, second_copies[1])
+    wait_all(second_handed)
+    feed(far, diag, (far_a, spare_a), (far_b, spare_b))
+    second.near(1, spare_a[...])
+    reduced.ps[1] = low(spare_b[...])
+    second.across(lambda part: far_a[part])
+    reduced.near(0)
+    reduced.near(1)
+
+    class LineSum:
+        def __init__(self, gw, yr, zr, za):
+            self.gw, self.yr, self.zr, self.za = gw, yr, zr, za
+            self.slot = whole(gw) if len(gw.shape) == 3 else inner(gw)
+            self.at = reserve(6)
+
+        def send(self, src, dst, device, i):
+            remote(src, dst, device, self.at + i).start()
+
+        def come(self, i):
+            part = self.zr.at[0]
+            remote(part, part, to_line(beside), self.at + i).wait_recv()
+
+        def along_y(self):
+            self.y_copies = [
+                push(self.slot(2 * i + 1 - y), self.yr.at[i], to_line(beside)) for i in range(4)
+            ]
+
+        def sum_y(self):
+            wait_all(self.y_copies)
+
+            def add(i, carry):
+                block = self.slot(2 * i + y)
+                block[...] = low(f32(block[...]) + f32(self.yr[i]))
+                return carry
+
+            lax.fori_loop(0, 4, add, 0)
+
+        def stage1(self):
+            @pl.when(is_end)
+            def _():
+                for i, place in enumerate(far_places + [partner]):
+                    self.send(self.slot(place), self.zr.at[i], to_line(partner), i)
+
+        def stage2(self):
+            @pl.when(is_middle)
+            def _():
+                for i, place in enumerate(far_places):
+                    self.come(i)
+                    block = self.slot(place)
+                    block[...] = low(f32(block[...]) + f32(self.zr[i]))
+                    self.send(block, self.za.at[i], to_line(facing), 3 + i)
+
+        def stage3(self):
+            @pl.when(is_middle)
+            def _():
+                for i in range(2):
+                    self.come(3 + i)
+                block = self.slot(partner)
+                block[...] = low(f32(block[...]) + f32(self.za[1 - lax.rem(z, 2)]))
+                self.send(block, self.zr.at[0], to_line(partner), 5)
+
+        def total(self, out):
+            own = f32(self.slot(s)[...])
+
+            @pl.when(is_middle)
+            def _():
+                self.come(2)
+                total = own + f32(self.zr[2]) + f32(self.za[lax.rem(z, 2)])
+                out[...] = total.astype(out.dtype)
+
+            @pl.when(is_end)
+            def _():
+                self.come(5)
+                out[...] = (own + f32(self.zr[0])).astype(out.dtype)
+
+        def sent(self):
+            part = self.zr.at[0]
+
+            def gone(i):
+                remote(part, part, to_line(beside), self.at + i).wait_send()
+
+            @pl.when(is_middle)
+            def _():
+                for i in (3, 4, 5):
+                    gone(i)
+
+            @pl.when(is_end)
+            def _():
+                for i in range(3):
+                    gone(i)
+
+    reduce_sum = LineSum(ref.gw_reduce, ref.yr_reduce, ref.zr_reduce, ref.za_reduce)
+    expand_sum = LineSum(ref.gw_expand, ref.yr_expand, ref.zr_expand, ref.za_expand)
+    output_sum = LineSum(ref.gw_output, ref.yr_output, ref.zr_output, ref.za_output)
+    joint_sum = LineSum(ref.gw_joint, ref.yr_joint, ref.zr_joint, ref.za_joint)
+    merge_sum = LineSum(ref.gw_merge, ref.yr_merge, ref.zr_merge, ref.za_merge)
+
+    gw_reduce = ref.gw_reduce
+
+    def reduce_block(j):
+        lhs = active_all[:, :, lanes(j * ROW, ROW)].reshape(TALL, ROW)
+        gw_reduce[j] = low(tn(lhs, tall(cot_all)))
+
+    def reduce_beside(i, carry):
+        reduce_block(2 * i + 1 - y)
+        return carry
+
+    def reduce_here(i, carry):
+        reduce_block(2 * i + y)
+        return carry
+
+    lax.fori_loop(0, 4, reduce_beside, 0)
+    reduce_sum.along_y()
+
+    csum = ref.csum
+
+    def note(i, value):
+        csum[i : i + 1] = jnp.sum(value, axis=0, keepdims=True)
+
+    grad_second = second.total(own_a[...])
+    grad_mid = ref.grad_mid
+    note(6, grad_second * ref.middle_hat[...])
+    note(7, grad_second)
+    grad_top = f32(ref.cot[...])
+    note(8, grad_top)
+    grad_mid[...] = grad_top + norm_back_ref(
+        grad_second, ref.middle_hat, ref.middle_inv, vector(SECOND_GAIN)
+    )
+    gb_all = ref.gb_all
+    gb_all[g] = low(grad_mid[...])
+    gb_copies = spread(gb_all)
+    note(5, f32(gb_all[g]))
+    lax.fori_loop(0, 4, reduce_here, 0)
+    gw_expand = ref.gw_expand
+
+    def expand_block(i, carry):
+        lhs = second_all[:, :, lanes(i * QC, QC)].reshape(TALL, QC)
+        gw_expand[i] = low(tn(lhs, tall(gh_all))).reshape(LINE, WD, D)
+        return carry
+
+    e12 = reserve(LINE)
+    g_send, go = ref.g_send, ref.go
+
+    def attended_back(i, j):
+        part = low(nt(two(gb_all, i, j), row_weight(output_s)))
+        for n, group in enumerate((i, j)):
+            for t in range(2):
+                g_send[group, t] = part[n * ROW : (n + 1) * ROW, t * 128 : (t + 1) * 128]
+                to_pair(g_send.at[group, t], go.at[line_rows, :], e12, group, t)
+
+    gb_copies[0].wait_recv()
+    attended_back(g, sib)
+    lax.fori_loop(0, 2, expand_block, 0)
+    gb_handed = spread_on(gb_all, gb_copies[1])
+    wait_all(gb_handed)
+    attended_back(far, diag)
+    reduced.across(lambda part: far_b[part])
+    lax.fori_loop(2, 4, expand_block, 0)
+    gw_output = ref.gw_output
+    gw_output[...] = low(tn(tall(att_all), tall(gb_all))).reshape(LINE, WD, D)
+    reduce_sum.sum_y()
+    expand_sum.along_y()
+    reduce_sum.stage1()
+    pairs_done(g_send.at[0, 0], go.at[line_rows, :], e12)
+
+    dk, dv, d_all = ref.dk, ref.dv, ref.d_all
+    dk[...] = jnp.zeros_like(dk)
+    dv[...] = jnp.zeros_like(dv)
+    e13 = reserve(LINE)
+
+    def attend_back_rows(b, carry):
+        here = rows(b * 256, 256)
+        queries = qkv[0, here, :]
+        keys, values = qkv[1], qkv[2]
+        grad = go[here]
+        products = f32(grad) * att_f[here]
+        outs = []
+        for t in range(2):
+            mine_lanes = half_of_lane == t
+            offset = jnp.sum(jnp.where(mine_lanes, products, 0.0), axis=-1, keepdims=True)
+            grad_t = low(jnp.where(mine_lanes, f32(grad), 0.0))
+            query_t = low(jnp.where(mine_lanes, f32(queries), 0.0))
+            weights = p_low[t, here, :]
+            slopes = low(low(f32(weights) * (nt(grad_t, values) - offset)) * SCALE)
+            outs.append(nn(slopes, keys))
+            dk[...] += tn(slopes, query_t)
+            dv[...] += tn(weights, grad_t)
+        grad_queries = low(jnp.where(half_of_lane == 0, outs[0], outs[1]))
+        pair_send[pl.ds(2 * b, 2), 0] = grad_queries.reshape(2, ROW, 128)
+        for t in range(2):
+            there = 2 * b + t
+            index = e13 + lax.rem(there - s + LINE, LINE)
+            src = pair_send.at[there, 0]
+            dst = d_all.at[mine, 0, :, pair_lanes]
+
+            @pl.when(there != s)
+            def _():
+                remote(src, dst, to_line(there), index).start()
+
+            @pl.when(there == s)
+            def _():
+                pltpu.make_async_copy(src, dst, recv.at[index]).start()
+
+        return carry
+
+    lax.fori_loop(0, GROUP // 256, attend_back_rows, 0)
+    pair_send[:, 1] = low(dk[...]).reshape(LINE, ROW, 128)
+    pair_send[:, 2] = low(dv[...]).reshape(LINE, ROW, 128)
+    d_copies = []
+    d_dst = d_all.at[mine, pl.ds(1, 2), :, pair_lanes]
+    for step in range(1, LINE):
+        there = lax.rem(s + step, LINE)
+        d_copies.append(push(pair_send.at[there, pl.ds(1, 2)], d_dst, to_line(there)))
+    d_here = pltpu.make_async_copy(
+        pair_send.at[s, pl.ds(1, 2)], d_dst, recv.at[reserve(1)]
+    )
+    d_here.start()
+    d_here.wait()
+    wait_all(d_copies)
+    pairs_done(pair_send.at[0, 0], d_all.at[mine, 0, :, pair_lanes], e13)
+    output_sum.along_y()
+    reduce_sum.stage2()
+
+    normed = TeamSum(sums.normed)
+
+    def joint_back(j):
+        total = None
+        for kind in range(3):
+            weight = joint_s[:, :, :, kind * QC : (kind + 1) * QC].reshape(D, QC)
+            part = nt(d_all[j, kind], weight)
+            total = part if total is None else total + part
+        return total
+
+    normed.near(1, joint_back(diag))
+    normed.near(0, joint_back(sib))
+    far_a[...] = joint_back(far)
+    normed.across(lambda part: far_a[part])
+    own_a[...] = joint_back(g)
+    gw_joint = ref.gw_joint
+    tsum = ref.tsum
+    for kind in range(3):
+        block = d_all[:, kind].reshape(TALL, QC)
+        for i in range(TEAM):
+            lhs = normed_all[:, :, i * QC : (i + 1) * QC].reshape(TALL, QC)
+            part = low(tn(lhs, block)).reshape(LINE, WD, QC)
+            gw_joint[i, :, :, kind * QC : (kind + 1) * QC] = part
+        if kind != 1:
+            row = 16 + kind // 2
+            tsum[s, row : row + 1] = jnp.sum(f32(block), axis=0, keepdims=True)
+    joint_sum.along_y()
+    expand_sum.sum_y()
+    expand_sum.stage1()
+    hidden_sums = jnp.sum(f32(tall(gh_all)), axis=0, keepdims=True)
+    for i in range(4):
+        tsum[s, 18 + i : 19 + i] = hidden_sums[:, i * QC : (i + 1) * QC]
+    tsum[s, 22:24] = jnp.zeros((2, QC), F32)
+
+    grad_normed = normed.total(own_a[...])
+    note(3, grad_normed * ref.start_hat[...])
+    note(4, grad_normed)
+    grad_start = grad_mid[...] + norm_back_ref(
+        grad_normed, ref.start_hat, ref.start_inv, vector(FIRST_GAIN)
+    )
+    gm_all = ref.gm_all
+    gm_all[g] = low(grad_start)
+    gm_copies = spread(gm_all)
+    note(0, f32(gm_all[g]))
+    note(1, lead * grad_start)
+    note(2, grad_start)
+    csum[9:16] = jnp.zeros((7, D), F32)
+    crecv = ref.crecv
+    crecv[g] = csum[:, lanes(g * QC, QC)]
+    c_copies = [
+        push(csum.at[:, lanes(j * QC, QC)], crecv.at[g], to_team(j)) for j in (far, diag, sib)
+    ]
+    ref.activations[...] = (
+        reduced.total(own_b[...]) + middle_ref[...] + vector(REDUCE_BIAS)
+    )
+    deposit(ref.activations, results.activations)
+    output_sum.sum_y()
+    output_sum.stage1()
+    reduce_sum.stage3()
+    gm_handed = spread_on(gm_all, gm_copies[1])
+    gm_copies[0].wait_recv()
+    wait_all(gm_handed)
+
+    gw_merge = ref.gw_merge
+    f_own = ref.f_own
+    t_send = ref.t_send
+    q_all = ref.q_all
+    grad_heads = low(nt(tall(gm_all), row_weight(merge_s)))
+    head_grad = ref.att_all
+    head_grad[...] = grad_heads.reshape(TEAM, ROW, QC)
+    q_all[s] = jnp.zeros((8, KP), F32)
+
+    def choose_back(h):
+        field = f32(tall(field_all))
+        grad_h = low(jnp.where(head_of_lane == h, f32(tall(head_grad)), 0.0))
+        value_back = nn(grad_h, pv[...].reshape(QC, KP))
+        grad_chosen = split_dot(value_back * field, select[...])
+        weights = chosen[h]
+        shifted = grad_chosen - jnp.sum(weights * grad_chosen, axis=-1, keepdims=True)
+        score_spread = nn(low(weights * shifted), select_t[...])
+        field_part = nn(low(weights), select_t[...]) * value_back + score_spread * probe[h : h + 1]
+        field_part = field_part.reshape(TEAM, ROW, KP)
+        if h == 0:
+            f_own[...] = field_part
+        else:
+            f_own[...] += field_part
+        q_all[s, h : h + 1] = jnp.sum(score_spread * field, axis=0, keepdims=True)
+
+    for h in range(TEAM_HEADS):
+        choose_back(h)
+        if h == 0:
+            expand_sum.stage2()
+        if h == 2:
+            joint_sum.sum_y()
+            joint_sum.stage1()
+    for h in range(TEAM_HEADS):
+        pair = tall(head_grad)[:, (h // 2) * 128 : (h // 2 + 1) * 128]
+        part = tn(pair, mixed[h])
+        at_row = (h % 2) * HDIM
+        t_send[2 * h : 2 * h + 2] = low(part[at_row : at_row + HDIM]).reshape(2, WD, KP)
+
+    t_recv = ref.t_recv
+    t_copies = []
+    for step in range(1, LINE):
+        there = lax.rem(s + step, LINE)
+        t_copies.append(push(t_send.at[there], t_recv.at[s], to_line(there)))
+    t_recv[s] = t_send[s]
+    q_copies = share_line(q_all.at[s], q_all.at[s])
+    gw_merge[...] = low(tn(head_low[...], tall(gm_all))).reshape(LINE, WD, D)
+    merge_sum.along_y()
+    f_recv = ref.f_recv
+    f_copies = []
+    for step in range(1, TEAM):
+        j = lax.rem(g + step, TEAM)
+        f_copies.append(push(f_own.at[j], f_recv.at[step - 1], to_team(j)))
+    output_sum.stage2()
+    wait_all(c_copies)
+    tsum[s, 0:16] = jnp.sum(crecv[...], axis=0)
+    s_copies = share_line(tsum.at[s], tsum.at[s])
+    position = jnp.zeros((ROW, QC), F32)
+    for j in range(TEAM):
+        position += f32(gm_all[j, :, lanes(g * QC, QC)])
+    ref.g_position[...] = position
+    deposit(ref.g_position, results.g_position)
+
+    wait_all(t_copies)
+    head_all, score_all = ref.head_all, ref.score_all
+    head_all[g, s] = low(jnp.sum(f32(t_recv[...]), axis=0))
+    h_copies = share_line(head_all.at[g, s], head_all.at[g, s])
+    wait_all(q_copies)
+    score_all[g] = jnp.sum(q_all[...], axis=0)
+    score_copies = [push(score_all.at[g], score_all.at[g], to_team(j)) for j in (far, diag, sib)]
+    merge_sum.sum_y()
+    merge_sum.stage1()
+    expand_sum.stage3()
+    output_sum.stage3()
+    joint_sum.stage2()
+    merge_sum.stage2()
+
+    xs_joint, xs_expand = ref.xs_joint, ref.xs_expand
+    xr_joint, xr_expand = ref.xr_joint, ref.xr_expand
+    expand_sum.total(xs_expand)
+    x_copies = []
+    for j in (far, diag, sib):
+        x_copies.append(push(xs_expand.at[j], xr_expand.at[g], to_team(j)))
+    xr_expand[g] = xs_expand[g]
+    joint_sum.stage3()
+    merge_sum.stage3()
+    joint_sum.total(xs_joint)
+    for j in (far, diag, sib):
+        x_copies.append(push(xs_joint.at[j], xr_joint.at[g], to_team(j)))
+    xr_joint[g] = xs_joint[g]
+    wait_all(h_copies)
+    h_spread = spread(head_all)
+    reduce_sum.total(ref.g_reduce)
+    deposit(ref.g_reduce, results.g_reduce)
+    output_sum.total(ref.g_output)
+    deposit(ref.g_output, results.g_output)
+    wait_all(f_copies)
+    ref.field_grad[...] = (f_own[g] + f_recv[0] + f_recv[1] + f_recv[2]).T[0:VP]
+    deposit(ref.field_grad, results.field_grad)
+    wait_all(s_copies)
+    ref.sums[...] = jnp.sum(tsum[...], axis=0)
+    h_handed = spread_on(head_all, h_spread[1])
+    merge_sum.total(ref.g_merge)
+    deposit(ref.g_merge, results.g_merge)
+    wait_all(x_copies)
+    for j in range(TEAM):
+        ref.g_expand[:, j * D : (j + 1) * D] = f32(xr_expand[j])
+        for kind in range(3):
+            at_lane = kind * D + j * QC
+            ref.g_joint[:, at_lane : at_lane + QC] = f32(
+                xr_joint[j, :, kind * QC : (kind + 1) * QC]
+            )
+    deposit(ref.g_expand, results.g_expand)
+    deposit(ref.g_joint, results.g_joint)
+    wait_all(score_copies)
+    score_rows = ref.score_rows
+    for j in range(TEAM):
+        score_rows[TEAM_HEADS * j : TEAM_HEADS * (j + 1)] = score_all[j, 0:TEAM_HEADS]
+
+    def exact(a, b, ca, cb):
+        return lax.dot_general(
+            a,
+            b,
+            (((ca,), (cb,)), ((), ())),
+            precision=lax.Precision.HIGHEST,
+            preferred_element_type=F32,
+        )
+
+    scores = score_rows[...]
+    query_row = vector(QUERY)
+    head_of = lax.broadcasted_iota(jnp.int32, (16, D), 1) // HDIM
+    head_rows = (head_of == lax.broadcasted_iota(jnp.int32, (16, D), 0)).astype(F32)
+    probe_own = f32(
+        low(exact(f32(ref.key_w[...]) * query_row, head_rows, 1, 1) * SCALE)
+    )
+    grad_probe = exact(f32(pe[...]), scores, 1, 1)
+    ref.g_key[...] = exact(grad_probe, head_rows, 1, 0) * (query_row * SCALE)
+    deposit(ref.g_key, results.g_key)
+    small = ref.small
+    picks = (
+        lax.broadcasted_iota(jnp.int32, (QC, 128), 0)
+        == lax.broadcasted_iota(jnp.int32, (QC, 128), 1) + s * WD
+    ) & (lax.broadcasted_iota(jnp.int32, (QC, 128), 1) < WD)
+    small[0:SUM_ROWS] = exact(ref.sums[...], picks.astype(F32), 1, 0)
+    hidden_row = jnp.zeros((1, QC), F32)
+    score_row = jnp.zeros((1, KP), F32)
+    own_scores = score_all[g]
+    for i in range(4):
+        hidden_row = jnp.where(s // 2 == i, ref.sums[18 + i : 19 + i], hidden_row)
+        score_row = jnp.where(s // 2 == i, own_scores[i : i + 1], score_row)
+    hidden_row = jnp.where(s % 2 == 0, hidden_row[:, 0:128], hidden_row[:, 128:256])
+    query_grad = exact(jnp.broadcast_to(score_row, (8, KP)), ref.key_own[...], 1, 1) * SCALE
+    small[24:32] = jnp.zeros((8, 128), F32)
+    small[24:25] = hidden_row
+    small[25:26, 0:WD] = query_grad[0:1]
+    deposit(small, results.small)
+    h_spread[0].wait_recv()
+    wait_all(h_handed)
+    heads = head_all[...].reshape(D, KP)
+    ref.g_value[...] = nt(pe[...], heads)
+    deposit(ref.g_value, results.g_value)
+    grad_table = nn(ref.value_w[...], heads) + exact(probe_own, scores, 1, 0)
+    ref.g_patch[...] = grad_table[:, 0:VP]
+    ref.g_embed[...] = grad_table[:, VP : VP + VARS]
+    deposit(ref.g_patch, results.g_patch)
+    deposit(ref.g_embed, results.g_embed)
+    for copy in begun:
+        copy.wait_send()
+    for gather in (gather_merge, gather_output, gather_reduce, gather_joint, gather_expand):
+        gather.sent()
+    for line_sum in (reduce_sum, expand_sum, output_sum, joint_sum, merge_sum):
+        line_sum.sent()
+    for copy in deposits:
+        copy.wait()
+
+
+def fused(operands):
+    scratch = list(SCRATCH.values()) + list(OUTPUTS.values())
+    for shape in TEAM_SUMS.values():
+        scratch += team_sum_buffers(shape)
+    return pl.pallas_call(
+        fused_kernel,
+        out_shape=[jax.ShapeDtypeStruct(*shape) for shape in OUTPUTS.values()],
+        in_specs=[pl.BlockSpec(memory_space=space) for space in INPUTS.values()],
+        out_specs=[pl.BlockSpec(memory_space=pl.ANY)] * len(OUTPUTS),
+        scratch_shapes=[pltpu.VMEM(*shape) for shape in scratch]
+        + [pltpu.SemaphoreType.DMA((SEMAPHORES,))] * 2,
+        compiler_params=pltpu.CompilerParams(
+            collective_id=1, has_side_effects=True, vmem_limit_bytes=64 << 20
+        ),
+    )(*operands)
+
+
+def hand_out_kernel(*refs):
+    n = (len(refs) - 2) // 3
+    arrays, results, held = refs[:n], refs[n : 2 * n], refs[2 * n : 3 * n]
+    came, left = refs[3 * n :]
+    fetches = [pltpu.make_async_copy(arrays[i], held[i], came.at[i]) for i in range(n)]
+    for copy in fetches:
+        copy.start()
+    stores = [pltpu.make_async_copy(held[i], results[i], left.at[i]) for i in range(n)]
+    for i in range(n):
+        fetches[i].wait()
+        stores[i].start()
+    for copy in stores:
+        copy.wait()
+
+
+def hand_out(arrays):
+    n = len(arrays)
+    return pl.pallas_call(
+        hand_out_kernel,
+        out_shape=[jax.ShapeDtypeStruct(a.shape, a.dtype) for a in arrays],
+        in_specs=[pl.BlockSpec(memory_space=pl.ANY)] * n,
+        out_specs=[pl.BlockSpec(memory_space=pl.ANY)] * n,
+        scratch_shapes=[pltpu.VMEM(a.shape, a.dtype) for a in arrays]
+        + [pltpu.SemaphoreType.DMA((n,))] * 2,
+        compiler_params=pltpu.CompilerParams(vmem_limit_bytes=64 << 20),
+    )(*arrays)
+
+
+def shards_fused(
+    fields,
+    patch_weight,
+    variable_embed,
+    query_vector,
+    key_weight,
+    value_weight,
+    merge_weight,
+    merge_bias,
+    position_table,
+    lead_weight,
+    lead_bias,
+    first_gain,
+    first_shift,
+    joint_weight,
+    joint_bias,
+    output_weight,
+    output_bias,
+    second_gain,
+    second_shift,
+    expand_weight,
+    expand_bias,
+    reduce_weight,
+    reduce_bias,
+    segment_ids,
+    live_rows,
+    lead_steps,
+    cotangent,
+):
+    vectors = jnp.stack(
+        [
+            query_vector,
+            merge_bias,
+            lead_weight,
+            lead_bias,
+            first_gain,
+            first_shift,
+            output_bias,
+            second_gain,
+            second_shift,
+            reduce_bias,
+            joint_bias[0],
+            joint_bias[1],
+        ]
+    )
+    wide = jnp.stack([expand_bias, low(segment_ids), low(live_rows)])
+    pack = jnp.concatenate(
+        [
+            jnp.pad(vectors, ((0, 16 - VECTORS), (0, 128 - WD))),
+            jnp.pad(wide, ((0, 13), (0, 0))),
+        ]
+    )
+    *whole, small = fused(
+        (
+            fields.T,
+            patch_weight.T,
+            variable_embed.T,
+            key_weight,
+            value_weight,
+            pack,
+            lead_steps,
+            cotangent,
+            position_table,
+            joint_weight,
+            expand_weight,
+            merge_weight,
+            output_weight,
+            reduce_weight,
+        )
+    )
+    (
+        activations,
+        field_grad,
+        g_patch,
+        g_embed,
+        g_key,
+        g_value,
+        g_merge,
+        g_position,
+        g_joint,
+        g_output,
+        g_expand,
+        g_reduce,
+    ) = hand_out(whole)
+    own = small[:, :WD]
+    return (
+        activations,
+        field_grad.T,
+        g_patch.T,
+        g_embed.T,
+        own[25],
+        g_key,
+        g_value,
+        g_merge,
+        own[0],
+        g_position,
+        own[1],
+        own[2],
+        own[3],
+        own[4],
+        g_joint,
+        own[16:18],
+        g_output,
+        own[5],
+        own[6],
+        own[7],
+        g_expand,
+        small[24],
+        g_reduce,
+        own[8],
+    )
+
+
 def solution(mesh):
     by_row = P(ROWS, None)
     by_column = P(None, ROWS)
@@ -662,5 +2013,12 @@
         by_row,
         vector,
     )
-    body = functools.partial(shards, mesh.shape["grp"], mesh.shape["seq"])
+    G, S = mesh.shape["grp"], mesh.shape["seq"]
+
+    def body(*args):
+        rows_here, weight_rows = args[0].shape[0], args[5].shape[0]
+        if (G, S, rows_here, weight_rows) == (TEAM, LINE, ROW, WD):
+            return shards_fused(*args)
+        return shards(G, S, *args)
+
     return jax.shard_map(body, mesh=mesh, in_specs=in_specs, out_specs=out_specs, check_vma=False)

time: 775 us -> 277 us (0.36); the launches traced: 765 us -> 277 us
  waiting for transfers between devices: 164 us -> 0 us
  local copies, waits for them, and re-layouts: 97.7 us -> 6.06 us
  matrix products: 83 us -> 0 us
  blocking collectives: 72.4 us -> 0 us
  other arithmetic: 42 us -> 0.62 us
  Pallas kernels: 290 us -> 269 us
  between operations: 16 us -> 0.94 us
    reduce_scatter x5 -> x0, waiting for transfers between devices: 162 us -> none  [the longest x2 108 us: scatter_mixed(): w = lax.psum_scatter(w, 'seq', scatter_dimension=0, tiled=False)]
    dot_general x41 -> x0, matrix products: 73.9 us -> none  [the longest x25 47.7 us: dot(): lax.dot_general(a, b, (((ca,), (cb,)), ((), ())), preferred_element_type=...]
    all_gather x2 -> x0, blocking collectives: 72.4 us -> none  [gather_rows(): return lax.all_gather(w, 'seq', axis=0, tiled=True)]
    reshape x26 -> x0, local copies, waits for them, and re-layouts: 32.5 us -> none  [the longest x4 9.18 us: to_pairs(): x = x.reshape(G, R, kinds, split, width).transpose(0, 3, 1, 2, 4)]
    reduce_sum x28 -> x0, other arithmetic: 22.4 us -> none  [the longest x1 2.43 us: shards(): jnp.sum(grad_normed, axis=0)]
    pallas_call x19 -> x2, Pallas kernels: 290 us -> 269 us  [the longest x1 266 us: fused(): pl.pallas_call(fused_kernel, out_shape=[jax.ShapeDtypeStruct(*shape) for...]
    convert_element_type x10 -> x0, other arithmetic: 10.3 us -> none  [the longest x6 5.49 us: f32(): return x.astype(F32)]
    transpose x12 -> x0, local copies, waits for them, and re-layouts: 9.62 us -> none  [the longest x2 2.74 us: scatter_mixed(): w.reshape(G, S, dn, cols).transpose(1, 0, 2, 3)]
  transfers between devices with their start and end apart: 8 -> 0, of which waited for: 3 -> 0; matrix products, arithmetic and copies ran while one was open for 22% -> 0% of each run, Pallas kernels for 26% -> 0%
where the time goes in v1:
time: 277 us
  Pallas kernels  269 us (97%)
  local copies, waits for them, and re-layouts  6.06 us (2%)
    pallas_call x1, Pallas kernels, fused(): pl.pallas_call(fused_kernel, out_shape=[jax.ShapeDtypeStruct(*shape) for...  266 us

profile of v1, /device:TPU:0, one launch (start us, length us, event | category | flops | bytes accessed | tf_op | source)
XLA Modules:
  0.0 276.6 jit_solution(13379810480579792968)
XLA Ops:
  0.7 0.6 copy-done.11
  1.3 0.0 copy-done.12
  1.3 0.7 copy-done.13
  2.0 0.0 copy-start.4
  2.0 0.0 copy-start.7
  2.1 0.0 copy-start.8
  2.1 0.5 copy-done
  2.6 0.0 copy-done.1
  2.7 0.0 copy-done.2
  2.7 0.0 copy-done.3
  2.7 0.0 copy-done.4
  2.7 0.0 copy-done.5
  2.7 0.0 copy-done.6
  2.7 0.0 copy-done.7
  2.8 0.0 copy-done.8
  2.8 0.0 copy-done.9
  2.8 0.0 copy-done.10
  2.8 0.1 stack.56
  2.9 0.6 fusion.1.refs_5_
  3.5 266.2 %shard_map.442 = (f32[128,1024]{1,0:T(8,128)}, f32[192,128]{1,0:T(8,128)}, f32[32,192]{1,0:T(8,128)}, f32[32,48]{1,0:T(8,128)}, f32[32,1024]{1,0:T(8,128)}, /*in...) custom-call(bf16[192,128]{1,0:T(8,128)(2,1)} %bitcast.43, ...), custom_call_target="tpu_custom_call" | custom-call | tf_op jit(solution)/shard_map/pallas_call | solution.py:1803
  269.7 2.8 %shard_map.443 = (f32[128,1024]{1,0:T(8,128)}, f32[192,128]{1,0:T(8,128)}, f32[32,192]{1,0:T(8,128)}, f32[32,48]{1,0:T(8,128)}, f32[32,1024]{1,0:T(8,128)}, /*in...) custom-call(f32[128,1024]{1,0:T(8,128)} %get-tuple-element.49.refs_0, ...), custom_call_target="tpu_custom_call" | custom-call | tf_op jit(solution)/shard_map/pallas_call | solution.py:1833
  272.5 1.2 slice_bitcast_fusion.1
  273.7 1.2 slice.57
  274.9 1.5 slice_bitcast_fusion
  (13 shorter events, 0.0 us)
Async XLA Ops:
  0.7 0.7 copy-start.11
  0.7 0.7 copy-start.12
  1.3 0.7 copy-start.13
  2.0 0.7 copy-start
  2.0 0.7 copy-start.1
  2.0 0.7 copy-start.2
  2.0 0.7 copy-start.3
  2.0 0.7 copy-start.4
  2.0 0.7 copy-start.5
  2.0 0.7 copy-start.6
  2.0 0.7 copy-start.7
  2.1 0.7 copy-start.8
  2.1 0.7 copy-start.9
  2.1 0.7 copy-start.10
